TPU v7x, 768 devices: a whole 4x8x12 slice. The times are simulated.
768 devices in a mesh: outer: 12 (over z), inner: 64 (over x, y, core).
Axes of the slice: x: 4, y: 8, z: 12, core: 2. Of those that a mesh axis runs over, the one named last changes fastest.
Arguments:
- queries: bfloat16 [196608, 1024], P(('outer', 'inner')), may hold values from -60 to 60
- key_states: bfloat16 [196608, 128], P(('outer', 'inner')), may hold values from -6 to 6
- value_states: bfloat16 [196608, 128], P(('outer', 'inner')), may hold values from -6 to 6
- grad_output: bfloat16 [196608, 1024], P(('outer', 'inner')), may hold values from -6 to 6
- documents: int32 [196608], replicated, may hold values from 0 to 511, never falling along the last dimension, each value on 1 to 768 neighbouring positions
- block_order: int32 [1536], replicated, may hold values from 0 to 1535, as said below
Outputs:
- grad_queries: bfloat16 [196608, 1024], P(('outer', 'inner'))
- grad_keys: bfloat16 [196608, 128], P(('outer', 'inner'))
- grad_values: bfloat16 [196608, 128], P(('outer', 'inner'))
Inputs may be any that keep to these rules, and one draw needn't show every extreme that they name: `documents`: never falling along the sequence; every document has 1 to 768 positions and one has exactly 768. `block_order`: device d of the joined index outer, inner (d = outer * 64 + inner) holds stored blocks 2 * d and 2 * d + 1, which are sequence blocks d and 1535 - d in either order.
All inputs are finite; a program needn't handle non-finite values.
Results may differ from a plain program's by a relative error of at most 0.0049.
Values may be sent and summed in bfloat16 or wider, within the bound.
A program may use at most 32 MiB of HBM per device.

v0:
```python
import math

import jax
import jax.numpy as jnp
from jax import lax
from jax.sharding import PartitionSpec as P

REACH = 6


NEGATIVE = -1e30


def padded(block, sides, width):
    for axis, dim in sides:
        count = lax.axis_size(axis)
        forward = [(i, i + 1) for i in range(count - 1)]
        backward = [(target, source) for source, target in forward]
        low = lax.ppermute(
            lax.slice_in_dim(block, block.shape[dim] - width, None, axis=dim), axis, forward
        )
        high = lax.ppermute(lax.slice_in_dim(block, 0, width, axis=dim), axis, backward)
        block = jnp.concatenate([low, block, high], axis=dim)
    return block


def stack_two(first_item, second_item):
    return jnp.stack([first_item, second_item])


def take_block(block_rows, slot_index, length):
    return lax.dynamic_slice_in_dim(block_rows, slot_index * length, length, 0)


def split_heads(block_rows, head_size):
    return block_rows.reshape(block_rows.shape[0], block_rows.shape[1] // head_size, head_size)


def allowed_pairs(documents, query_block, key_block, length):
    offsets = jnp.arange(length, dtype=jnp.int32)
    query_place = query_block * length + offsets
    key_place = key_block * length + offsets
    query_owner = lax.dynamic_slice_in_dim(documents, query_block * length, length, 0)
    key_owner = lax.dynamic_slice_in_dim(documents, jnp.maximum(key_block, 0) * length, length, 0)
    same_owner = key_owner[None, :] == query_owner[:, None]
    return (key_block >= 0) & (key_place[None, :] <= query_place[:, None]) & same_owner


def forward_blocks(extended, first_block, length, at_top):
    from_above = extended[extended.shape[0] - length :]
    return (extended[:length], jnp.where(at_top, first_block, from_above))


def send_back(carried, length, at_top, stashed=None):
    extended = padded(
        jnp.concatenate([carried[0], carried[1]], 0), ((("outer", "inner"), 0),), length
    )
    new_second = extended[:length]
    new_first = jnp.where(at_top, carried[1], extended[extended.shape[0] - length :])
    return stack_two(new_first, new_second)


def apply_pairs(update, allowed_sets, operands):
    return jax.vmap(update)(allowed_sets, *operands)


def on_device(queries, key_states, value_states, grad_output, documents, block_order):
    axis_count = lax.axis_size(("outer", "inner"))
    device = lax.axis_index(("outer", "inner"))
    length = key_states.shape[0] // 2
    head_size = key_states.shape[1]
    factor = 1.0 / math.sqrt(head_size)
    slot_zero = block_order[2 * device]
    slot_one = block_order[2 * device + 1]
    first_slot = jnp.where(slot_zero < axis_count, 0, 1).astype(jnp.int32)
    second_slot = 1 - first_slot
    first_block = jnp.minimum(slot_zero, slot_one)
    second_block = jnp.maximum(slot_zero, slot_one)
    at_top = device == axis_count - 1
    joined = jnp.concatenate([key_states, value_states], 1)
    moving = (take_block(joined, first_slot, length), take_block(joined, second_slot, length))
    query_pair = stack_two(
        split_heads(take_block(queries, first_slot, length), head_size),
        split_heads(take_block(queries, second_slot, length), head_size),
    )
    output_pair = stack_two(
        split_heads(take_block(grad_output, first_slot, length), head_size),
        split_heads(take_block(grad_output, second_slot, length), head_size),
    )
    head_count = query_pair.shape[2]

    def pair_scores(query_heads, output_heads, pair_blocks):
        key_part = pair_blocks[:, :head_size]
        value_part = pair_blocks[:, head_size:]
        scores = (
            jnp.einsum("bhd,wd->hbw", query_heads, key_part, preferred_element_type=jnp.float32)
            * factor
        )
        grad_prob = jnp.einsum(
            "bhd,wd->hbw", output_heads, value_part, preferred_element_type=jnp.float32
        )
        return (scores, grad_prob)

    def stats_update(
        allowed, running_max, totals, weighted, query_heads, output_heads, pair_blocks
    ):
        scores, grad_prob = pair_scores(query_heads, output_heads, pair_blocks)
        masked = jnp.where(allowed[None], scores, NEGATIVE)
        new_max = jnp.maximum(running_max, masked.max(-1))
        rescale = jnp.exp(running_max - new_max)
        weights = jnp.where(allowed[None], jnp.exp(scores - new_max[..., None]), 0.0)
        return (
            new_max,
            totals * rescale + weights.sum(-1),
            weighted * rescale + (weights * grad_prob).sum(-1),
        )

    def grad_update(allowed, query_heads, output_heads, pair_blocks, log_totals, row_dots):
        scores, grad_prob = pair_scores(query_heads, output_heads, pair_blocks)
        probabilities = jnp.where(allowed[None], jnp.exp(scores - log_totals[..., None]), 0.0)
        grad_scores = probabilities * (grad_prob - row_dots[..., None])
        rounded_probs = probabilities.astype(jnp.bfloat16)
        rounded_grads = grad_scores.astype(jnp.bfloat16)
        grad_rows = jnp.einsum(
            "hbw,wd->bhd",
            rounded_grads,
            pair_blocks[:, :head_size],
            preferred_element_type=jnp.float32,
        )
        grad_key = jnp.einsum(
            "hbw,bhd->wd", rounded_grads, query_heads, preferred_element_type=jnp.float32
        )
        grad_value = jnp.einsum(
            "hbw,bhd->wd", rounded_probs, output_heads, preferred_element_type=jnp.float32
        )
        return (grad_rows, jnp.concatenate([grad_key, grad_value], 1))

    def pair_masks(offset):
        return stack_two(
            allowed_pairs(documents, first_block, first_block - offset, length),
            allowed_pairs(documents, second_block, second_block - offset, length),
        )

    blank_stats = jnp.zeros((2, head_count, length), jnp.float32)
    running = (jnp.full((2, head_count, length), NEGATIVE, jnp.float32), blank_stats, blank_stats)
    received = []
    for offset in range(REACH + 1):
        if offset > 0:
            extended = padded(
                jnp.concatenate([moving[1], moving[0]], 0), ((("outer", "inner"), 0),), length
            )
            moving = forward_blocks(extended, moving[0], length, at_top)
        received.append(stack_two(moving[0], moving[1]))
        running = apply_pairs(
            stats_update, pair_masks(offset), running + (query_pair, output_pair, received[offset])
        )
    log_totals = running[0] + jnp.log(running[1])
    row_dots = running[2] / running[1]
    shared = (query_pair, output_pair)
    grad_total = jnp.zeros(query_pair.shape, jnp.float32)
    for offset in range(REACH, -1, -1):
        grad_part, contribution = apply_pairs(
            grad_update, pair_masks(offset), shared + (received[offset], log_totals, row_dots)
        )
        grad_total = grad_total + grad_part
        carried = (
            contribution if offset == REACH else send_back(carried, length, at_top) + contribution
        )
    grad_query = (
        (grad_total * factor).astype(jnp.bfloat16).reshape(2, length, head_count * head_size)
    )
    grad_key = (carried[:, :, :head_size] * factor).astype(jnp.bfloat16)
    grad_value = carried[:, :, head_size:].astype(jnp.bfloat16)

    def restore(paired):
        return jnp.concatenate([paired[first_slot], paired[second_slot]], 0)

    return (restore(grad_query), restore(grad_key), restore(grad_value))


def solution(mesh):
    in_specs = (
        P(("outer", "inner"), None),
        P(("outer", "inner"), None),
        P(("outer", "inner"), None),
        P(("outer", "inner"), None),
        P(),
        P(),
    )
    out_specs = (
        P(("outer", "inner"), None),
        P(("outer", "inner"), None),
        P(("outer", "inner"), None),
    )
    return jax.shard_map(
        on_device, mesh=mesh, in_specs=in_specs, out_specs=out_specs, check_vma=False
    )
```

profile of v0, /device:TPU:512, one launch (start us, length us, event | category | flops | bytes accessed | tf_op | source)
XLA Modules:
  0.0 200.6 jit_solution(4699262843759380956)
XLA Ops:
  4.4 8.2 %collective-permute-start.6 = (bf16[128,256]{1,0:T(8,128)(2,1)S(1)}, bf16[128,256]{1,0:T(8,128)(2,1)S(1)}, u32[]{:S(2)}, u32[]{:S(2)}) collective-permute-start(bf16[128,256]{1,0:T(8,128)(2,1)S(1)} %constant_dynamic-slice_fusion.6), channel_id=1, source_target_pairs={{1,0},{2,1},{3,2},{4,3},{5,4},{6,5},{7,6},{8,7},{9,8},{10,9},{11,1... | collective-permute-start | bytes 196616 | tf_op jit(solution)/shard_map/ppermute | solution.py:22
  22.3 9.1 %collective-permute-start.7 = (bf16[128,256]{1,0:T(8,128)(2,1)S(1)}, bf16[128,256]{1,0:T(8,128)(2,1)S(1)}, u32[]{:S(2)}, u32[]{:S(2)}) collective-permute-start(bf16[128,256]{1,0:T(8,128)(2,1)S(1)} %get-tuple-element.27), channel_id=1, source_target_pairs={{1,0},{2,1},{3,2},{4,3},{5,4},{6,5},{7,6},{8,7},{9,8},{10,9},{11,1... | collective-permute-start | bytes 196616 | tf_op jit(solution)/shard_map/ppermute | solution.py:22
  33.3 9.1 %collective-permute-start.8 = (bf16[128,256]{1,0:T(8,128)(2,1)S(1)}, bf16[128,256]{1,0:T(8,128)(2,1)S(1)}, u32[]{:S(2)}, u32[]{:S(2)}) collective-permute-start(bf16[128,256]{1,0:T(8,128)(2,1)S(1)} %broadcast_select_fusion.3), channel_id=1, source_target_pairs={{1,0},{2,1},{3,2},{4,3},{5,4},{6,5},{7,6},{8,7},{9,8},{10,9},{11,1... | collective-permute-start | bytes 196616 | tf_op jit(solution)/shard_map/ppermute | solution.py:22
  44.7 8.8 %collective-permute-done.1 = bf16[128,256]{1,0:T(8,128)(2,1)S(1)} collective-permute-done((bf16[128,256]{1,0:T(8,128)(2,1)S(1)}, bf16[128,256]{1,0:T(8,128)(2,1)S(1)}, u32[]{:S(2)}, u32[]{:S(2)}) %collective-permute-start.1) | collective-permute-done | bytes 65568 | tf_op jit(solution)/shard_map/ppermute | solution.py:19
  55.4 2.4 %collective-permute-start.2 = (bf16[128,256]{1,0:T(8,128)(2,1)S(1)}, bf16[128,256]{1,0:T(8,128)(2,1)S(1)}, u32[]{:S(2)}, u32[]{:S(2)}) collective-permute-start(bf16[128,256]{1,0:T(8,128)(2,1)S(1)} %collective-permute-done.1), channel_id=1, source_target_pairs={{0,1},{1,2},{2,3},{3,4},{4,5},{5,6},{6,7},{7,8},{8,9},{9,10},{10,1... | collective-permute-start | bytes 196616 | tf_op jit(solution)/shard_map/ppermute | solution.py:19
  58.1 8.3 %collective-permute-done.2 = bf16[128,256]{1,0:T(8,128)(2,1)S(1)} collective-permute-done((bf16[128,256]{1,0:T(8,128)(2,1)S(1)}, bf16[128,256]{1,0:T(8,128)(2,1)S(1)}, u32[]{:S(2)}, u32[]{:S(2)}) %collective-permute-start.2) | collective-permute-done | bytes 65568 | tf_op jit(solution)/shard_map/ppermute | solution.py:19
  68.3 2.4 %collective-permute-start.3 = (bf16[128,256]{1,0:T(8,128)(2,1)S(1)}, bf16[128,256]{1,0:T(8,128)(2,1)S(1)}, u32[]{:S(2)}, u32[]{:S(2)}) collective-permute-start(bf16[128,256]{1,0:T(8,128)(2,1)S(1)} %collective-permute-done.2), channel_id=1, source_target_pairs={{0,1},{1,2},{2,3},{3,4},{4,5},{5,6},{6,7},{7,8},{8,9},{9,10},{10,1... | collective-permute-start | bytes 196616 | tf_op jit(solution)/shard_map/ppermute | solution.py:19
  71.1 8.3 %collective-permute-done.3 = bf16[128,256]{1,0:T(8,128)(2,1)S(1)} collective-permute-done((bf16[128,256]{1,0:T(8,128)(2,1)S(1)}, bf16[128,256]{1,0:T(8,128)(2,1)S(1)}, u32[]{:S(2)}, u32[]{:S(2)}) %collective-permute-start.3) | collective-permute-done | bytes 65568 | tf_op jit(solution)/shard_map/ppermute | solution.py:19
  81.3 2.4 %collective-permute-start.4 = (bf16[128,256]{1,0:T(8,128)(2,1)S(1)}, bf16[128,256]{1,0:T(8,128)(2,1)S(1)}, u32[]{:S(2)}, u32[]{:S(2)}) collective-permute-start(bf16[128,256]{1,0:T(8,128)(2,1)S(1)} %collective-permute-done.3), channel_id=1, source_target_pairs={{0,1},{1,2},{2,3},{3,4},{4,5},{5,6},{6,7},{7,8},{8,9},{9,10},{10,1... | collective-permute-start | bytes 196616 | tf_op jit(solution)/shard_map/ppermute | solution.py:19
  84.0 8.3 %collective-permute-done.4 = bf16[128,256]{1,0:T(8,128)(2,1)S(1)} collective-permute-done((bf16[128,256]{1,0:T(8,128)(2,1)S(1)}, bf16[128,256]{1,0:T(8,128)(2,1)S(1)}, u32[]{:S(2)}, u32[]{:S(2)}) %collective-permute-start.4) | collective-permute-done | bytes 65568 | tf_op jit(solution)/shard_map/ppermute | solution.py:19
  94.6 9.1 %collective-permute-done.5 = bf16[128,256]{1,0:T(8,128)(2,1)S(1)} collective-permute-done((bf16[128,256]{1,0:T(8,128)(2,1)S(1)}, bf16[128,256]{1,0:T(8,128)(2,1)S(1)}, u32[]{:S(2)}, u32[]{:S(2)}) %collective-permute-start.5) | collective-permute-done | bytes 65568 | tf_op jit(solution)/shard_map/ppermute | solution.py:19
  110.5 2.1 %collective-permute-start.12 = (f32[128,256]{1,0:T(8,128)S(1)}, f32[128,256]{1,0:T(8,128)S(1)}, u32[]{:S(2)}, u32[]{:S(2)}) collective-permute-start(f32[128,256]{1,0:T(8,128)S(1)} %fusion.54), channel_id=1, source_target_pairs={{1,0},{2,1},{3,2},{4,3},{5,4},{6,5},{7,6},{8,7},{9,8},{10,9},{11,1... | collective-permute-start | bytes 393224 | tf_op jit(solution)/shard_map/ppermute | solution.py:22
  116.6 2.4 %collective-permute-start.13 = (f32[128,256]{1,0:T(8,128)S(1)}, f32[128,256]{1,0:T(8,128)S(1)}, u32[]{:S(2)}, u32[]{:S(2)}) collective-permute-start(f32[128,256]{1,0:T(8,128)S(1)} %get-tuple-element.18), channel_id=1, source_target_pairs={{0,1},{1,2},{2,3},{3,4},{4,5},{5,6},{6,7},{7,8},{8,9},{9,10},{10,1... | collective-permute-start | bytes 393224 | tf_op jit(solution)/shard_map/ppermute | solution.py:19
  119.3 9.0 %collective-permute-done.13 = f32[128,256]{1,0:T(8,128)S(1)} collective-permute-done((f32[128,256]{1,0:T(8,128)S(1)}, f32[128,256]{1,0:T(8,128)S(1)}, u32[]{:S(2)}, u32[]{:S(2)}) %collective-permute-start.13) | collective-permute-done | bytes 131104 | tf_op jit(solution)/shard_map/ppermute | solution.py:19
  130.6 2.4 %collective-permute-start.15 = (f32[128,256]{1,0:T(8,128)S(1)}, f32[128,256]{1,0:T(8,128)S(1)}, u32[]{:S(2)}, u32[]{:S(2)}) collective-permute-start(f32[128,256]{1,0:T(8,128)S(1)} %get-tuple-element.60), channel_id=1, source_target_pairs={{0,1},{1,2},{2,3},{3,4},{4,5},{5,6},{6,7},{7,8},{8,9},{9,10},{10,1... | collective-permute-start | bytes 393224 | tf_op jit(solution)/shard_map/ppermute | solution.py:19
  133.1 9.3 %collective-permute-done.15 = f32[128,256]{1,0:T(8,128)S(1)} collective-permute-done((f32[128,256]{1,0:T(8,128)S(1)}, f32[128,256]{1,0:T(8,128)S(1)}, u32[]{:S(2)}, u32[]{:S(2)}) %collective-permute-start.15) | collective-permute-done | bytes 131104 | tf_op jit(solution)/shard_map/ppermute | solution.py:19
  144.6 2.4 %collective-permute-start.17 = (f32[128,256]{1,0:T(8,128)S(1)}, f32[128,256]{1,0:T(8,128)S(1)}, u32[]{:S(2)}, u32[]{:S(2)}) collective-permute-start(f32[128,256]{1,0:T(8,128)S(1)} %get-tuple-element.58), channel_id=1, source_target_pairs={{0,1},{1,2},{2,3},{3,4},{4,5},{5,6},{6,7},{7,8},{8,9},{9,10},{10,1... | collective-permute-start | bytes 393224 | tf_op jit(solution)/shard_map/ppermute | solution.py:19
  147.1 9.3 %collective-permute-done.17 = f32[128,256]{1,0:T(8,128)S(1)} collective-permute-done((f32[128,256]{1,0:T(8,128)S(1)}, f32[128,256]{1,0:T(8,128)S(1)}, u32[]{:S(2)}, u32[]{:S(2)}) %collective-permute-start.17) | collective-permute-done | bytes 131104 | tf_op jit(solution)/shard_map/ppermute | solution.py:19
  158.6 2.4 %collective-permute-start.19 = (f32[128,256]{1,0:T(8,128)S(1)}, f32[128,256]{1,0:T(8,128)S(1)}, u32[]{:S(2)}, u32[]{:S(2)}) collective-permute-start(f32[128,256]{1,0:T(8,128)S(1)} %get-tuple-element.56), channel_id=1, source_target_pairs={{0,1},{1,2},{2,3},{3,4},{4,5},{5,6},{6,7},{7,8},{8,9},{9,10},{10,1... | collective-permute-start | bytes 393224 | tf_op jit(solution)/shard_map/ppermute | solution.py:19
  161.1 9.3 %collective-permute-done.19 = f32[128,256]{1,0:T(8,128)S(1)} collective-permute-done((f32[128,256]{1,0:T(8,128)S(1)}, f32[128,256]{1,0:T(8,128)S(1)}, u32[]{:S(2)}, u32[]{:S(2)}) %collective-permute-start.19) | collective-permute-done | bytes 131104 | tf_op jit(solution)/shard_map/ppermute | solution.py:19
  172.6 2.4 %collective-permute-start.21 = (f32[128,256]{1,0:T(8,128)S(1)}, f32[128,256]{1,0:T(8,128)S(1)}, u32[]{:S(2)}, u32[]{:S(2)}) collective-permute-start(f32[128,256]{1,0:T(8,128)S(1)} %get-tuple-element.54), channel_id=1, source_target_pairs={{0,1},{1,2},{2,3},{3,4},{4,5},{5,6},{6,7},{7,8},{8,9},{9,10},{10,1... | collective-permute-start | bytes 393224 | tf_op jit(solution)/shard_map/ppermute | solution.py:19
  175.1 9.3 %collective-permute-done.21 = f32[128,256]{1,0:T(8,128)S(1)} collective-permute-done((f32[128,256]{1,0:T(8,128)S(1)}, f32[128,256]{1,0:T(8,128)S(1)}, u32[]{:S(2)}, u32[]{:S(2)}) %collective-permute-start.21) | collective-permute-done | bytes 131104 | tf_op jit(solution)/shard_map/ppermute | solution.py:19
  187.5 2.4 %collective-permute-start.23 = (f32[128,256]{1,0:T(8,128)S(1)}, f32[128,256]{1,0:T(8,128)S(1)}, u32[]{:S(2)}, u32[]{:S(2)}) collective-permute-start(f32[128,256]{1,0:T(8,128)S(1)} %get-tuple-element.52), channel_id=1, source_target_pairs={{0,1},{1,2},{2,3},{3,4},{4,5},{5,6},{6,7},{7,8},{8,9},{9,10},{10,1... | collective-permute-start | bytes 393224 | tf_op jit(solution)/shard_map/ppermute | solution.py:19
  189.9 9.3 %collective-permute-done.23 = f32[128,256]{1,0:T(8,128)S(1)} collective-permute-done((f32[128,256]{1,0:T(8,128)S(1)}, f32[128,256]{1,0:T(8,128)S(1)}, u32[]{:S(2)}, u32[]{:S(2)}) %collective-permute-start.23) | collective-permute-done | bytes 131104 | tf_op jit(solution)/shard_map/ppermute | solution.py:19
  (135 shorter events, 47.3 us)
Async XLA Ops:
  4.4 15.9 %collective-permute-start.6 = (bf16[128,256]{1,0:T(8,128)(2,1)S(1)}, bf16[128,256]{1,0:T(8,128)(2,1)S(1)}, u32[]{:S(2)}, u32[]{:S(2)}) collective-permute-start(bf16[128,256]{1,0:T(8,128)(2,1)S(1)} %constant_dynamic-slice_fusion.6), channel_id=1, source_target_pairs={{1,0},{2,1},{3,2},{4,3},{5,4},{6,5},{7,6},{8,7},{9,8},{10,9},{11,1... | collective-permute-start | bytes 196616 | tf_op jit(solution)/shard_map/ppermute | solution.py:22
  20.4 11.3 %collective-permute-start = (bf16[128,256]{1,0:T(8,128)(2,1)S(1)}, bf16[128,256]{1,0:T(8,128)(2,1)S(1)}, u32[]{:S(2)}, u32[]{:S(2)}) collective-permute-start(bf16[128,256]{1,0:T(8,128)(2,1)S(1)} %get-tuple-element.28), channel_id=1, source_target_pairs={{0,1},{1,2},{2,3},{3,4},{4,5},{5,6},{6,7},{7,8},{8,9},{9,10},{10,1... | collective-permute-start | bytes 196616 | tf_op jit(solution)/shard_map/ppermute | solution.py:19
  22.3 11.0 %collective-permute-start.7 = (bf16[128,256]{1,0:T(8,128)(2,1)S(1)}, bf16[128,256]{1,0:T(8,128)(2,1)S(1)}, u32[]{:S(2)}, u32[]{:S(2)}) collective-permute-start(bf16[128,256]{1,0:T(8,128)(2,1)S(1)} %get-tuple-element.27), channel_id=1, source_target_pairs={{1,0},{2,1},{3,2},{4,3},{5,4},{6,5},{7,6},{8,7},{9,8},{10,9},{11,1... | collective-permute-start | bytes 196616 | tf_op jit(solution)/shard_map/ppermute | solution.py:22
  33.3 11.4 %collective-permute-start.8 = (bf16[128,256]{1,0:T(8,128)(2,1)S(1)}, bf16[128,256]{1,0:T(8,128)(2,1)S(1)}, u32[]{:S(2)}, u32[]{:S(2)}) collective-permute-start(bf16[128,256]{1,0:T(8,128)(2,1)S(1)} %broadcast_select_fusion.3), channel_id=1, source_target_pairs={{1,0},{2,1},{3,2},{4,3},{5,4},{6,5},{7,6},{8,7},{9,8},{10,9},{11,1... | collective-permute-start | bytes 196616 | tf_op jit(solution)/shard_map/ppermute | solution.py:22
  42.4 11.0 %collective-permute-start.1 = (bf16[128,256]{1,0:T(8,128)(2,1)S(1)}, bf16[128,256]{1,0:T(8,128)(2,1)S(1)}, u32[]{:S(2)}, u32[]{:S(2)}) collective-permute-start(bf16[128,256]{1,0:T(8,128)(2,1)S(1)} %collective-permute-done), channel_id=1, source_target_pairs={{0,1},{1,2},{2,3},{3,4},{4,5},{5,6},{6,7},{7,8},{8,9},{9,10},{10,1... | collective-permute-start | bytes 196616 | tf_op jit(solution)/shard_map/ppermute | solution.py:19
  53.5 12.9 %collective-permute-start.9 = (bf16[128,256]{1,0:T(8,128)(2,1)S(1)}, bf16[128,256]{1,0:T(8,128)(2,1)S(1)}, u32[]{:S(2)}, u32[]{:S(2)}) collective-permute-start(bf16[128,256]{1,0:T(8,128)(2,1)S(1)} %broadcast_select_fusion.2), channel_id=1, source_target_pairs={{1,0},{2,1},{3,2},{4,3},{5,4},{6,5},{7,6},{8,7},{9,8},{10,9},{11,1... | collective-permute-start | bytes 196616 | tf_op jit(solution)/shard_map/ppermute | solution.py:22
  55.4 11.0 %collective-permute-start.2 = (bf16[128,256]{1,0:T(8,128)(2,1)S(1)}, bf16[128,256]{1,0:T(8,128)(2,1)S(1)}, u32[]{:S(2)}, u32[]{:S(2)}) collective-permute-start(bf16[128,256]{1,0:T(8,128)(2,1)S(1)} %collective-permute-done.1), channel_id=1, source_target_pairs={{0,1},{1,2},{2,3},{3,4},{4,5},{5,6},{6,7},{7,8},{8,9},{9,10},{10,1... | collective-permute-start | bytes 196616 | tf_op jit(solution)/shard_map/ppermute | solution.py:19
  66.4 12.9 %collective-permute-start.10 = (bf16[128,256]{1,0:T(8,128)(2,1)S(1)}, bf16[128,256]{1,0:T(8,128)(2,1)S(1)}, u32[]{:S(2)}, u32[]{:S(2)}) collective-permute-start(bf16[128,256]{1,0:T(8,128)(2,1)S(1)} %broadcast_select_fusion.1), channel_id=1, source_target_pairs={{1,0},{2,1},{3,2},{4,3},{5,4},{6,5},{7,6},{8,7},{9,8},{10,9},{11,1... | collective-permute-start | bytes 196616 | tf_op jit(solution)/shard_map/ppermute | solution.py:22
  68.3 11.0 %collective-permute-start.3 = (bf16[128,256]{1,0:T(8,128)(2,1)S(1)}, bf16[128,256]{1,0:T(8,128)(2,1)S(1)}, u32[]{:S(2)}, u32[]{:S(2)}) collective-permute-start(bf16[128,256]{1,0:T(8,128)(2,1)S(1)} %collective-permute-done.2), channel_id=1, source_target_pairs={{0,1},{1,2},{2,3},{3,4},{4,5},{5,6},{6,7},{7,8},{8,9},{9,10},{10,1... | collective-permute-start | bytes 196616 | tf_op jit(solution)/shard_map/ppermute | solution.py:19
  79.4 15.2 %collective-permute-start.11 = (bf16[128,256]{1,0:T(8,128)(2,1)S(1)}, bf16[128,256]{1,0:T(8,128)(2,1)S(1)}, u32[]{:S(2)}, u32[]{:S(2)}) collective-permute-start(bf16[128,256]{1,0:T(8,128)(2,1)S(1)} %broadcast_select_fusion), channel_id=1, source_target_pairs={{1,0},{2,1},{3,2},{4,3},{5,4},{6,5},{7,6},{8,7},{9,8},{10,9},{11,1... | collective-permute-start | bytes 196616 | tf_op jit(solution)/shard_map/ppermute | solution.py:22
  81.3 11.0 %collective-permute-start.4 = (bf16[128,256]{1,0:T(8,128)(2,1)S(1)}, bf16[128,256]{1,0:T(8,128)(2,1)S(1)}, u32[]{:S(2)}, u32[]{:S(2)}) collective-permute-start(bf16[128,256]{1,0:T(8,128)(2,1)S(1)} %collective-permute-done.3), channel_id=1, source_target_pairs={{0,1},{1,2},{2,3},{3,4},{4,5},{5,6},{6,7},{7,8},{8,9},{9,10},{10,1... | collective-permute-start | bytes 196616 | tf_op jit(solution)/shard_map/ppermute | solution.py:19
  92.6 11.0 %collective-permute-start.5 = (bf16[128,256]{1,0:T(8,128)(2,1)S(1)}, bf16[128,256]{1,0:T(8,128)(2,1)S(1)}, u32[]{:S(2)}, u32[]{:S(2)}) collective-permute-start(bf16[128,256]{1,0:T(8,128)(2,1)S(1)} %collective-permute-done.4), channel_id=1, source_target_pairs={{0,1},{1,2},{2,3},{3,4},{4,5},{5,6},{6,7},{7,8},{8,9},{9,10},{10,1... | collective-permute-start | bytes 196616 | tf_op jit(solution)/shard_map/ppermute | solution.py:19
  110.5 6.1 %collective-permute-start.12 = (f32[128,256]{1,0:T(8,128)S(1)}, f32[128,256]{1,0:T(8,128)S(1)}, u32[]{:S(2)}, u32[]{:S(2)}) collective-permute-start(f32[128,256]{1,0:T(8,128)S(1)} %fusion.54), channel_id=1, source_target_pairs={{1,0},{2,1},{3,2},{4,3},{5,4},{6,5},{7,6},{8,7},{9,8},{10,9},{11,1... | collective-permute-start | bytes 393224 | tf_op jit(solution)/shard_map/ppermute | solution.py:22
  116.6 11.7 %collective-permute-start.13 = (f32[128,256]{1,0:T(8,128)S(1)}, f32[128,256]{1,0:T(8,128)S(1)}, u32[]{:S(2)}, u32[]{:S(2)}) collective-permute-start(f32[128,256]{1,0:T(8,128)S(1)} %get-tuple-element.18), channel_id=1, source_target_pairs={{0,1},{1,2},{2,3},{3,4},{4,5},{5,6},{6,7},{7,8},{8,9},{9,10},{10,1... | collective-permute-start | bytes 393224 | tf_op jit(solution)/shard_map/ppermute | solution.py:19
  128.4 4.6 %collective-permute-start.14 = (f32[128,256]{1,0:T(8,128)S(1)}, f32[128,256]{1,0:T(8,128)S(1)}, u32[]{:S(2)}, u32[]{:S(2)}) collective-permute-start(f32[128,256]{1,0:T(8,128)S(1)} %get-tuple-element.59), channel_id=1, source_target_pairs={{1,0},{2,1},{3,2},{4,3},{5,4},{6,5},{7,6},{8,7},{9,8},{10,9},{11,1... | collective-permute-start | bytes 393224 | tf_op jit(solution)/shard_map/ppermute | solution.py:22
  130.6 11.7 %collective-permute-start.15 = (f32[128,256]{1,0:T(8,128)S(1)}, f32[128,256]{1,0:T(8,128)S(1)}, u32[]{:S(2)}, u32[]{:S(2)}) collective-permute-start(f32[128,256]{1,0:T(8,128)S(1)} %get-tuple-element.60), channel_id=1, source_target_pairs={{0,1},{1,2},{2,3},{3,4},{4,5},{5,6},{6,7},{7,8},{8,9},{9,10},{10,1... | collective-permute-start | bytes 393224 | tf_op jit(solution)/shard_map/ppermute | solution.py:19
  142.4 4.6 %collective-permute-start.16 = (f32[128,256]{1,0:T(8,128)S(1)}, f32[128,256]{1,0:T(8,128)S(1)}, u32[]{:S(2)}, u32[]{:S(2)}) collective-permute-start(f32[128,256]{1,0:T(8,128)S(1)} %get-tuple-element.57), channel_id=1, source_target_pairs={{1,0},{2,1},{3,2},{4,3},{5,4},{6,5},{7,6},{8,7},{9,8},{10,9},{11,1... | collective-permute-start | bytes 393224 | tf_op jit(solution)/shard_map/ppermute | solution.py:22
  144.6 11.7 %collective-permute-start.17 = (f32[128,256]{1,0:T(8,128)S(1)}, f32[128,256]{1,0:T(8,128)S(1)}, u32[]{:S(2)}, u32[]{:S(2)}) collective-permute-start(f32[128,256]{1,0:T(8,128)S(1)} %get-tuple-element.58), channel_id=1, source_target_pairs={{0,1},{1,2},{2,3},{3,4},{4,5},{5,6},{6,7},{7,8},{8,9},{9,10},{10,1... | collective-permute-start | bytes 393224 | tf_op jit(solution)/shard_map/ppermute | solution.py:19
  156.4 4.6 %collective-permute-start.18 = (f32[128,256]{1,0:T(8,128)S(1)}, f32[128,256]{1,0:T(8,128)S(1)}, u32[]{:S(2)}, u32[]{:S(2)}) collective-permute-start(f32[128,256]{1,0:T(8,128)S(1)} %get-tuple-element.55), channel_id=1, source_target_pairs={{1,0},{2,1},{3,2},{4,3},{5,4},{6,5},{7,6},{8,7},{9,8},{10,9},{11,1... | collective-permute-start | bytes 393224 | tf_op jit(solution)/shard_map/ppermute | solution.py:22
  158.6 11.7 %collective-permute-start.19 = (f32[128,256]{1,0:T(8,128)S(1)}, f32[128,256]{1,0:T(8,128)S(1)}, u32[]{:S(2)}, u32[]{:S(2)}) collective-permute-start(f32[128,256]{1,0:T(8,128)S(1)} %get-tuple-element.56), channel_id=1, source_target_pairs={{0,1},{1,2},{2,3},{3,4},{4,5},{5,6},{6,7},{7,8},{8,9},{9,10},{10,1... | collective-permute-start | bytes 393224 | tf_op jit(solution)/shard_map/ppermute | solution.py:19
  170.4 4.6 %collective-permute-start.20 = (f32[128,256]{1,0:T(8,128)S(1)}, f32[128,256]{1,0:T(8,128)S(1)}, u32[]{:S(2)}, u32[]{:S(2)}) collective-permute-start(f32[128,256]{1,0:T(8,128)S(1)} %get-tuple-element.53), channel_id=1, source_target_pairs={{1,0},{2,1},{3,2},{4,3},{5,4},{6,5},{7,6},{8,7},{9,8},{10,9},{11,1... | collective-permute-start | bytes 393224 | tf_op jit(solution)/shard_map/ppermute | solution.py:22
  172.6 11.7 %collective-permute-start.21 = (f32[128,256]{1,0:T(8,128)S(1)}, f32[128,256]{1,0:T(8,128)S(1)}, u32[]{:S(2)}, u32[]{:S(2)}) collective-permute-start(f32[128,256]{1,0:T(8,128)S(1)} %get-tuple-element.54), channel_id=1, source_target_pairs={{0,1},{1,2},{2,3},{3,4},{4,5},{5,6},{6,7},{7,8},{8,9},{9,10},{10,1... | collective-permute-start | bytes 393224 | tf_op jit(solution)/shard_map/ppermute | solution.py:19
  184.4 5.5 %collective-permute-start.22 = (f32[128,256]{1,0:T(8,128)S(1)}, f32[128,256]{1,0:T(8,128)S(1)}, u32[]{:S(2)}, u32[]{:S(2)}) collective-permute-start(f32[128,256]{1,0:T(8,128)S(1)} %get-tuple-element.51), channel_id=1, source_target_pairs={{1,0},{2,1},{3,2},{4,3},{5,4},{6,5},{7,6},{8,7},{9,8},{10,9},{11,1... | collective-permute-start | bytes 393224 | tf_op jit(solution)/shard_map/ppermute | solution.py:22
  187.5 11.7 %collective-permute-start.23 = (f32[128,256]{1,0:T(8,128)S(1)}, f32[128,256]{1,0:T(8,128)S(1)}, u32[]{:S(2)}, u32[]{:S(2)}) collective-permute-start(f32[128,256]{1,0:T(8,128)S(1)} %get-tuple-element.52), channel_id=1, source_target_pairs={{0,1},{1,2},{2,3},{3,4},{4,5},{5,6},{6,7},{7,8},{8,9},{9,10},{10,1... | collective-permute-start | bytes 393224 | tf_op jit(solution)/shard_map/ppermute | solution.py:19
  (1 other events, 14.8 us)
where the time goes:
time: 202 us; the launch traced here: 201 us
  waiting for transfers between devices  99.6 us (49%)
  starting transfers between devices  71.3 us (35%)
  matrix products  11.7 us (6%)
  local copies, waits for them, and re-layouts  7.39 us (4%)
  other arithmetic  5.48 us (3%)
  between operations  5.19 us (3%)
    ppermute x12, waiting for transfers between devices, padded(): lax.ppermute(lax.slice_in_dim(block, block.shape[dim] - width, None, axis...  98 us
    ppermute x12, starting transfers between devices, padded(): lax.ppermute(lax.slice_in_dim(block, 0, width, axis=dim), axis, backward)  43.9 us
    ppermute x12, starting transfers between devices, padded(): lax.ppermute(lax.slice_in_dim(block, block.shape[dim] - width, None, axis...  27.4 us
  transfers between devices with their start and end apart: 24, of which 12 were waited for; matrix products, arithmetic and copies ran while one was open for 7% of the time, Pallas kernels for 0%

commit v1 on v0

v1 whole, which is shorter than its diff:
```python
import functools
import math

import jax
import jax.numpy as jnp
from jax import lax
from jax.experimental import pallas as pl
from jax.experimental.pallas import tpu as pltpu
from jax.sharding import PartitionSpec as P

BLK = 128
PAIR = 2 * BLK
D = 128
HEADS = 8
WIDE = HEADS * D
COLS = 2 * HEADS * BLK
NEGATIVE = -1e30
FACTOR = 1.0 / math.sqrt(D)
TO_EXP2 = FACTOR * math.log2(math.e)
MESH = pl.DeviceIdType.MESH
F32 = jnp.float32
BF16 = jnp.bfloat16


def dot_last(a, b):
    return lax.dot_general(a, b, (((1,), (1,)), ((), ())), preferred_element_type=F32)


def dot_mid(a, b):
    return lax.dot_general(a, b, (((1,), (0,)), ((), ())), preferred_element_type=F32)


def rows_of(j, half):
    if j == 0 and half == 1:
        return BLK, BLK
    if j == 3 and half == 0:
        return 0, BLK
    return 0, PAIR


def kernel(
    count,
    inner,
    order_ref,
    docs_ref,
    q_ref,
    k_ref,
    v_ref,
    do_ref,
    dq_ref,
    dk_ref,
    dv_ref,
    q_in,
    do_in,
    k_in,
    v_in,
    docs_in,
    q_all,
    do_all,
    q_other,
    do_other,
    kv,
    kv_other,
    bias,
    weights,
    grad_prob,
    st_max,
    st_sum,
    st_dot,
    st_scale,
    st_row,
    probs,
    grads,
    key_t,
    g_send,
    g_mine,
    g_other,
    own_grad,
    sib_send,
    sib_recv,
    dq_send,
    dq_recv,
    dq_mine,
    in_sem,
    kv_send_sem,
    kv_recv_sem,
    sib_send_sem,
    sib_recv_sem,
    g_send_sem,
    g_recv_sem,
):
    device = lax.axis_index("outer") * inner + lax.axis_index("inner")
    chip = lax.div(device, 2)
    core = lax.rem(device, 2)
    worker = chip + core * (count - 1 - 2 * chip)
    mirror = count - 1 - worker

    def place(u):
        u = lax.rem(u + count, count)
        upper = lax.div(u, count // 2)
        return 2 * u + upper * (2 * count - 1 - 4 * u)

    def coords(dev):
        return (lax.div(dev, inner), lax.rem(dev, inner))

    after = [place(worker + k) for k in (1, 2, 3)]
    before = [place(worker - k) for k in (1, 2, 3)]
    across = [place(mirror + k) for k in (1, 2, 3)]
    sibling = place(mirror)

    first_row = jnp.maximum(2 * worker - 6, 0)
    loads = [
        pltpu.make_async_copy(k_ref, k_in, in_sem.at[0]),
        pltpu.make_async_copy(v_ref, v_in, in_sem.at[1]),
        pltpu.make_async_copy(q_ref, q_in, in_sem.at[2]),
        pltpu.make_async_copy(do_ref, do_in, in_sem.at[3]),
        pltpu.make_async_copy(docs_ref.at[pl.ds(first_row, 8)], docs_in, in_sem.at[4]),
    ]
    for load in loads:
        load.start()

    barrier = pltpu.get_barrier_semaphore()
    for dev in after + before + [sibling]:
        pl.semaphore_signal(barrier, inc=1, device_id=coords(dev), device_id_type=MESH)
    for dev in across:

        @pl.when(dev != device)
        def _():
            pl.semaphore_signal(barrier, inc=1, device_id=coords(dev), device_id_type=MESH)

    own_hits = sum((dev == device).astype(jnp.int32) for dev in across)

    slot_zero = order_ref[2 * device]
    low_first = (slot_zero < count).astype(jnp.int32)
    keeps_zero = jnp.full((8, 128), low_first + core) == 1

    def choose(first, second):
        flat = keeps_zero[:1, :1]
        return jnp.where(flat, first, second), jnp.where(flat, second, first)

    loads[0].wait()
    mine, other = choose(k_in[:BLK], k_in[BLK:])
    kv[3 * PAIR : 3 * PAIR + BLK, :D] = mine
    kv_other[:, :D] = other
    loads[1].wait()
    mine, other = choose(v_in[:BLK], v_in[BLK:])
    kv[3 * PAIR : 3 * PAIR + BLK, D:] = mine
    kv_other[:, D:] = other

    pl.semaphore_wait(barrier, 10 - own_hits)

    def kv_mine_copy(k):
        start = (3 - k) * PAIR
        return pltpu.make_async_remote_copy(
            src_ref=kv.at[pl.ds(3 * PAIR, BLK)],
            dst_ref=kv.at[pl.ds(start, BLK)],
            send_sem=kv_send_sem.at[2 * k],
            recv_sem=kv_recv_sem.at[2 * k],
            device_id=coords(after[k - 1]),
            device_id_type=MESH,
        )

    def kv_other_copy(k):
        start = (3 - k) * PAIR + BLK
        return pltpu.make_async_remote_copy(
            src_ref=kv_other,
            dst_ref=kv.at[pl.ds(start, BLK)],
            send_sem=kv_send_sem.at[2 * k + 1],
            recv_sem=kv_recv_sem.at[2 * k + 1],
            device_id=coords(across[k - 1] if k else sibling),
            device_id_type=MESH,
        )

    kv_other_copy(0).start()
    for k in (1, 2, 3):
        kv_mine_copy(k).start()
        dev = across[k - 1]

        @pl.when(dev != device)
        def _():
            kv_other_copy(k).start()

        @pl.when(dev == device)
        def _():
            pltpu.make_async_copy(
                kv_other,
                kv.at[pl.ds((3 - k) * PAIR + BLK, BLK)],
                kv_recv_sem.at[2 * k + 1],
            ).start()

    loads[2].wait()
    for h in range(HEADS):
        lanes = slice(h * D, (h + 1) * D)
        mine, other = choose(q_in[:BLK, lanes], q_in[BLK:, lanes])
        q_all[h * BLK : (h + 1) * BLK] = mine
        q_other[h * BLK : (h + 1) * BLK] = other
    loads[3].wait()
    for h in range(HEADS):
        lanes = slice(h * D, (h + 1) * D)
        mine, other = choose(do_in[:BLK, lanes], do_in[BLK:, lanes])
        do_all[h * BLK : (h + 1) * BLK] = mine
        do_other[h * BLK : (h + 1) * BLK] = other

    def to_sibling(src, dst, index):
        return pltpu.make_async_remote_copy(
            src_ref=src,
            dst_ref=dst,
            send_sem=sib_send_sem.at[index],
            recv_sem=sib_recv_sem.at[index],
            device_id=coords(sibling),
            device_id_type=MESH,
        )

    q_move = to_sibling(q_other, q_all.at[pl.ds(COLS // 2, COLS // 2)], 0)
    do_move = to_sibling(do_other, do_all.at[pl.ds(COLS // 2, COLS // 2)], 1)
    q_move.start()
    do_move.start()

    loads[4].wait()
    key_iota = lax.broadcasted_iota(jnp.int32, (BLK, BLK), 0)
    query_iota = lax.broadcasted_iota(jnp.int32, (BLK, BLK), 1)

    def doc_row(window_block):
        block = 2 * worker - 6 + window_block
        return docs_in[jnp.maximum(block, 0) - first_row]

    query_docs = [jnp.broadcast_to(doc_row(6 + half), (BLK, BLK)) for half in (0, 1)]
    for block in range(8):
        key_docs = jnp.broadcast_to(doc_row(block).astype(F32), (BLK, BLK)).T.astype(jnp.int32)
        key_docs = jnp.where(2 * worker - 6 + block >= 0, key_docs, -1)
        for half in (0, 1):
            if block < half or block > 6 + half:
                continue
            allowed = key_docs == query_docs[half]
            if block == 6 + half:
                allowed = allowed & (key_iota <= query_iota)
            if block == half:
                allowed = allowed & (key_iota > query_iota)
            bias[half, block * BLK : (block + 1) * BLK] = jnp.where(allowed, 0.0, NEGATIVE)

    def scores(j, half):
        first, rows = rows_of(j, half)
        begin = j * PAIR + first

        def step(i, carry):
            t = half * 4 + i
            lanes = pl.ds(pl.multiple_of(t * PAIR, PAIR), PAIR)
            mask = bias[half, begin : begin + rows]
            s = dot_last(kv[begin : begin + rows, :D], q_all[lanes])
            s = s + jnp.concatenate([mask, mask], 1)
            g = dot_last(kv[begin : begin + rows, D:], do_all[lanes])
            top = jnp.max(s, axis=0, keepdims=True)
            e = jnp.exp2((s - top) * TO_EXP2)
            weights[j, t, first : first + rows] = e
            grad_prob[j, t, first : first + rows] = g
            st_max[j, t] = jnp.broadcast_to(top, (8, PAIR))
            st_sum[j, t] = jnp.sum(e.reshape(rows // 8, 8, PAIR), axis=0)
            st_dot[j, t] = jnp.sum((e * g).reshape(rows // 8, 8, PAIR), axis=0)
            return carry

        lax.fori_loop(0, 4, step, 0)

    def transpose_keys(j, first, rows):
        begin = j * PAIR + first
        key_t[:, begin : begin + rows] = kv[begin : begin + rows, :D].astype(F32).T.astype(BF16)

    scores(3, 0)
    transpose_keys(3, 0, BLK)
    kv_other_copy(0).wait_recv()
    q_move.wait_recv()
    do_move.wait_recv()
    scores(3, 1)
    transpose_keys(3, BLK, BLK)
    for j in (2, 1, 0):
        k = 3 - j
        kv_mine_copy(k).wait_recv()
        kv_other_copy(k).wait_recv()
        scores(j, 0)
        scores(j, 1)
        transpose_keys(j, 0, PAIR)

    def finish_stats(t, carry):
        tops = [st_max[j, t] for j in range(4)]
        top = jnp.maximum(jnp.maximum(tops[0], tops[1]), jnp.maximum(tops[2], tops[3]))
        scales = [jnp.exp2((tops[j] - top) * TO_EXP2) for j in range(4)]
        total = sum(st_sum[j, t] * scales[j] for j in range(4))
        dotted = sum(st_dot[j, t] * scales[j] for j in range(4))
        inverse = 1.0 / jnp.sum(total, axis=0, keepdims=True)
        row = jnp.sum(dotted, axis=0, keepdims=True) * inverse
        for j in range(4):
            st_scale[j, t] = scales[j] * inverse
        st_row[t] = jnp.broadcast_to(row, (8, PAIR))
        return carry

    lax.fori_loop(0, 8, finish_stats, 0)

    def grads_of(j):
        for half in (0, 1):
            first, rows = rows_of(j, half)

            def step(i, carry):
                t = half * 4 + i
                lanes = pl.ds(pl.multiple_of(t * PAIR, PAIR), PAIR)
                tall = (rows // 8, 8, PAIR)
                p = weights[j, t, first : first + rows].reshape(tall) * st_scale[j, t][None]
                g = grad_prob[j, t, first : first + rows].reshape(tall) - st_row[t][None]
                ds = (p * g).reshape(rows, PAIR)
                probs[first : first + rows, lanes] = p.reshape(rows, PAIR).astype(BF16)
                grads[j * PAIR + first : j * PAIR + first + rows, lanes] = ds.astype(BF16)
                return carry

            lax.fori_loop(0, 4, step, 0)

    def key_value_grads(j):
        if j in (1, 2):
            parts = [(0, PAIR, 0, COLS)]
        elif j == 0:
            parts = [(0, BLK, 0, COLS // 2), (BLK, BLK, 0, COLS)]
        else:
            parts = [(0, BLK, 0, COLS), (BLK, BLK, COLS // 2, COLS // 2)]
        for first, rows, lane, lanes in parts:
            begin = j * PAIR + first
            gk = dot_mid(grads[begin : begin + rows, lane : lane + lanes], q_all[lane : lane + lanes])
            gv = dot_mid(probs[first : first + rows, lane : lane + lanes], do_all[lane : lane + lanes])
            if j < 3:
                g_send[2 - j, first : first + rows, :D] = gk.astype(BF16)
                g_send[2 - j, first : first + rows, D:] = gv.astype(BF16)
            elif first == 0:
                own_grad[:, :D] = gk
                own_grad[:, D:] = gv
            else:
                sib_send[:, :D] = gk
                sib_send[:, D:] = gv

    def g_mine_copy(k):
        return pltpu.make_async_remote_copy(
            src_ref=g_send.at[k - 1, pl.ds(0, BLK)],
            dst_ref=g_mine.at[k - 1],
            send_sem=g_send_sem.at[2 * k - 2],
            recv_sem=g_recv_sem.at[2 * k - 2],
            device_id=coords(before[k - 1]),
            device_id_type=MESH,
        )

    def g_other_copy(k):
        return pltpu.make_async_remote_copy(
            src_ref=g_send.at[k - 1, pl.ds(BLK, BLK)],
            dst_ref=g_other.at[k - 1],
            send_sem=g_send_sem.at[2 * k - 1],
            recv_sem=g_recv_sem.at[2 * k - 1],
            device_id=coords(across[k - 1]),
            device_id_type=MESH,
        )

    for j in (0, 1, 2):
        k = 3 - j
        grads_of(j)
        key_value_grads(j)
        g_mine_copy(k).start()
        dev = across[k - 1]

        @pl.when(dev != device)
        def _():
            g_other_copy(k).start()

        @pl.when(dev == device)
        def _():
            pltpu.make_async_copy(
                g_send.at[k - 1, pl.ds(BLK, BLK)], g_other.at[k - 1], g_recv_sem.at[2 * k - 1]
            ).start()

    grads_of(3)
    key_value_grads(3)
    sib_move = to_sibling(sib_send, sib_recv, 2)
    sib_move.start()

    def query_grads(half, target):
        begin = half * BLK

        def step(i, carry):
            lanes = pl.ds(pl.multiple_of((half * 4 + i) * PAIR, PAIR), PAIR)
            g = dot_mid(key_t[:, begin : begin + 7 * BLK], grads[begin : begin + 7 * BLK, lanes])
            g = g * FACTOR
            for side in (0, 1):
                head = pl.ds(pl.multiple_of((i * 2 + side) * D, D), D)
                target[:, head] = g[:, side * BLK : (side + 1) * BLK].T.astype(BF16)
            return carry

        lax.fori_loop(0, 4, step, 0)

    query_grads(1, dq_send)
    dq_move = to_sibling(dq_send, dq_recv, 3)
    dq_move.start()
    query_grads(0, dq_mine)

    sib_move.wait_recv()
    dq_move.wait_recv()
    for h in range(HEADS):
        lanes = slice(h * D, (h + 1) * D)
        one, two = choose(dq_mine[:, lanes], dq_recv[:, lanes])
        dq_ref[:BLK, lanes] = one
        dq_ref[BLK:, lanes] = two

    mine_sum = own_grad[...]
    other_sum = sib_recv[...]
    for k in (3, 2, 1):
        g_mine_copy(k).wait_recv()
        g_other_copy(k).wait_recv()
        mine_sum = mine_sum + g_mine[k - 1].astype(F32)
        other_sum = other_sum + g_other[k - 1].astype(F32)
    one, two = choose(mine_sum, other_sum)
    dk_ref[:BLK] = (one[:, :D] * FACTOR).astype(BF16)
    dk_ref[BLK:] = (two[:, :D] * FACTOR).astype(BF16)
    dv_ref[:BLK] = one[:, D:].astype(BF16)
    dv_ref[BLK:] = two[:, D:].astype(BF16)

    kv_other_copy(0).wait_send()
    q_move.wait_send()
    do_move.wait_send()
    sib_move.wait_send()
    dq_move.wait_send()
    for k in (1, 2, 3):
        kv_mine_copy(k).wait_send()
        g_mine_copy(k).wait_send()

        @pl.when(across[k - 1] != device)
        def _():
            kv_other_copy(k).wait_send()
            g_other_copy(k).wait_send()


def on_device(queries, key_states, value_states, grad_output, documents, block_order):
    inner = lax.axis_size("inner")
    count = lax.axis_size("outer") * inner
    vmem = pl.BlockSpec(memory_space=pltpu.VMEM)
    hbm = pl.BlockSpec(memory_space=pl.ANY)
    docs = documents.reshape(2 * count, 1, BLK)
    return pl.pallas_call(
        functools.partial(kernel, count, inner),
        out_shape=[
            jax.ShapeDtypeStruct((PAIR, WIDE), BF16),
            jax.ShapeDtypeStruct((PAIR, D), BF16),
            jax.ShapeDtypeStruct((PAIR, D), BF16),
        ],
        in_specs=[pl.BlockSpec(memory_space=pltpu.SMEM)] + [hbm] * 5,
        out_specs=[vmem] * 3,
        scratch_shapes=[
            pltpu.VMEM((PAIR, WIDE), BF16),
            pltpu.VMEM((PAIR, WIDE), BF16),
            pltpu.VMEM((PAIR, D), BF16),
            pltpu.VMEM((PAIR, D), BF16),
            pltpu.VMEM((8, 1, BLK), jnp.int32),
            pltpu.VMEM((COLS, D), BF16),
            pltpu.VMEM((COLS, D), BF16),
            pltpu.VMEM((COLS // 2, D), BF16),
            pltpu.VMEM((COLS // 2, D), BF16),
            pltpu.VMEM((4 * PAIR, 2 * D), BF16),
            pltpu.VMEM((BLK, 2 * D), BF16),
            pltpu.VMEM((2, 4 * PAIR, BLK), F32),
            pltpu.VMEM((4, 8, PAIR, PAIR), F32),
            pltpu.VMEM((4, 8, PAIR, PAIR), F32),
            pltpu.VMEM((4, 8, 8, PAIR), F32),
            pltpu.VMEM((4, 8, 8, PAIR), F32),
            pltpu.VMEM((4, 8, 8, PAIR), F32),
            pltpu.VMEM((4, 8, 8, PAIR), F32),
            pltpu.VMEM((8, 8, PAIR), F32),
            pltpu.VMEM((PAIR, COLS), BF16),
            pltpu.VMEM((4 * PAIR, COLS), BF16),
            pltpu.VMEM((D, 4 * PAIR), BF16),
            pltpu.VMEM((3, PAIR, 2 * D), BF16),
            pltpu.VMEM((3, BLK, 2 * D), BF16),
            pltpu.VMEM((3, BLK, 2 * D), BF16),
            pltpu.VMEM((BLK, 2 * D), F32),
            pltpu.VMEM((BLK, 2 * D), F32),
            pltpu.VMEM((BLK, 2 * D), F32),
            pltpu.VMEM((BLK, WIDE), BF16),
            pltpu.VMEM((BLK, WIDE), BF16),
            pltpu.VMEM((BLK, WIDE), BF16),
            pltpu.SemaphoreType.DMA((5,)),
            pltpu.SemaphoreType.DMA((8,)),
            pltpu.SemaphoreType.DMA((8,)),
            pltpu.SemaphoreType.DMA((4,)),
            pltpu.SemaphoreType.DMA((4,)),
            pltpu.SemaphoreType.DMA((6,)),
            pltpu.SemaphoreType.DMA((6,)),
        ],
        compiler_params=pltpu.CompilerParams(
            collective_id=0, has_side_effects=True, vmem_limit_bytes=48 * 1024 * 1024
        ),
        name="attention_backward",
    )(block_order, docs, queries, key_states, value_states, grad_output)


def solution(mesh):
    rows = P(("outer", "inner"), None)
    return jax.shard_map(
        on_device,
        mesh=mesh,
        in_specs=(rows, rows, rows, rows, P(), P()),
        out_specs=(rows, rows, rows),
        check_vma=False,
    )
```

time: 202 us -> 49.9 us (0.25)
  the two profiles are of different devices: /device:TPU:512 before, /device:TPU:1 now
where the time goes in v1:
time: 49.9 us; the launch traced here: 49.5 us
  Pallas kernels  41.2 us (83%)
  local copies, waits for them, and re-layouts  7.64 us (15%)
  between operations  0.65 us (1%)
    pallas_call x1, Pallas kernels, on_device(): pl.pallas_call(functools.partial(kernel, count, inner), out_shape=[jax.Sh...  41.2 us
    unnamed x15, local copies, waits for them, and re-layouts  7.64 us

profile of v1, /device:TPU:1, one launch (start us, length us, event | category | flops | bytes accessed | tf_op | source)
XLA Modules:
  0.0 49.5 jit_solution(16193652525085528036)
XLA Ops:
  0.6 0.0 copy-start
  0.6 1.1 %copy-done = s32[196608]{0:T(1024)S(1)} copy-done((s32[196608]{0:T(1024)S(1)}, s32[196608]{0:T(1024)}, u32[]{:S(2)}) %copy-start) | copy-done | bytes 786456
  1.8 0.0 copy-start.1
  1.8 1.0 %copy-done.1 = bf16[256,1024]{1,0:T(8,128)(2,1)S(1)} copy-done((bf16[256,1024]{1,0:T(8,128)(2,1)S(1)}, bf16[256,1024]{1,0:T(8,128)(2,1)}, u32[]{:S(2)}) %copy-start.1) | copy-done | bytes 524312
  2.8 0.0 copy-start.2
  2.8 1.0 %copy-done.2 = bf16[256,1024]{1,0:T(8,128)(2,1)S(1)} copy-done((bf16[256,1024]{1,0:T(8,128)(2,1)S(1)}, bf16[256,1024]{1,0:T(8,128)(2,1)}, u32[]{:S(2)}) %copy-start.2) | copy-done | bytes 524312
  3.9 0.0 copy-start.3
  3.9 0.8 %copy-done.3 = bf16[256,128]{1,0:T(8,128)(2,1)S(1)} copy-done((bf16[256,128]{1,0:T(8,128)(2,1)S(1)}, bf16[256,128]{1,0:T(8,128)(2,1)}, u32[]{:S(2)}) %copy-start.3) | copy-done | bytes 65560
  4.7 0.0 copy-start.4
  4.7 0.8 %copy-done.4 = bf16[256,128]{1,0:T(8,128)(2,1)S(1)} copy-done((bf16[256,128]{1,0:T(8,128)(2,1)S(1)}, bf16[256,128]{1,0:T(8,128)(2,1)}, u32[]{:S(2)}) %copy-start.4) | copy-done | bytes 65560
  5.5 0.0 copy-start.5
  5.5 0.7 %copy-done.5 = s32[1536]{0:T(1024)S(1)} copy-done((s32[1536]{0:T(1024)S(1)}, s32[1536]{0:T(1024)}, u32[]{:S(2)}) %copy-start.5) | copy-done | bytes 6168
  6.2 41.2 %attention_backward.1 = (bf16[256,1024]{1,0:T(8,128)(2,1)S(1)}, bf16[256,128]{1,0:T(8,128)(2,1)S(1)}, bf16[256,128]{1,0:T(8,128)(2,1)S(1)}) custom-call(s32[1536]{0:T(1024)S(1)} %copy-done.5, s32[1536,1,128]{2,1,0:T(1,128)S(1)} %bitcast.1, bf16[256,1024]{1,0:T(8,128)(2,1)S(1)} %copy-done.1, bf16[256,128]{1,0:T(8,128)(2,1)S(1)} %copy-done.3, ...), custom_call_target="tpu_custom_call" | custom-call | tf_op jit(solution)/shard_map/attention_backward/pallas_call | solution.py:438
  47.5 0.8 %copy.12 = bf16[256,1024]{1,0:T(8,128)(2,1)} copy(bf16[256,1024]{1,0:T(8,128)(2,1)S(1)} %get-tuple-element.6) | data formatting | bytes 1048576
  48.3 0.6 %copy.13 = bf16[256,128]{1,0:T(8,128)(2,1)} copy(bf16[256,128]{1,0:T(8,128)(2,1)S(1)} %get-tuple-element.7) | data formatting | bytes 131072
  48.9 0.6 %copy.14 = bf16[256,128]{1,0:T(8,128)(2,1)} copy(bf16[256,128]{1,0:T(8,128)(2,1)S(1)} %get-tuple-element.8) | data formatting | bytes 131072
Async XLA Ops:
  0.6 1.1 %copy-start = (s32[196608]{0:T(1024)S(1)}, s32[196608]{0:T(1024)}, u32[]{:S(2)}) copy-start(s32[196608]{0:T(1024)} %param.10) | copy-start | bytes 2359300
  1.8 1.0 %copy-start.1 = (bf16[256,1024]{1,0:T(8,128)(2,1)S(1)}, bf16[256,1024]{1,0:T(8,128)(2,1)}, u32[]{:S(2)}) copy-start(bf16[256,1024]{1,0:T(8,128)(2,1)} %q_ref.1) | copy-start | bytes 1572868
  2.8 1.0 %copy-start.2 = (bf16[256,1024]{1,0:T(8,128)(2,1)S(1)}, bf16[256,1024]{1,0:T(8,128)(2,1)}, u32[]{:S(2)}) copy-start(bf16[256,1024]{1,0:T(8,128)(2,1)} %do_ref.1) | copy-start | bytes 1572868
  3.9 0.8 %copy-start.3 = (bf16[256,128]{1,0:T(8,128)(2,1)S(1)}, bf16[256,128]{1,0:T(8,128)(2,1)}, u32[]{:S(2)}) copy-start(bf16[256,128]{1,0:T(8,128)(2,1)} %k_ref.1) | copy-start | bytes 196612
  4.7 0.8 %copy-start.4 = (bf16[256,128]{1,0:T(8,128)(2,1)S(1)}, bf16[256,128]{1,0:T(8,128)(2,1)}, u32[]{:S(2)}) copy-start(bf16[256,128]{1,0:T(8,128)(2,1)} %v_ref.1) | copy-start | bytes 196612
  5.5 0.7 %copy-start.5 = (s32[1536]{0:T(1024)S(1)}, s32[1536]{0:T(1024)}, u32[]{:S(2)}) copy-start(s32[1536]{0:T(1024)} %order_ref.1) | copy-start | bytes 18436

commit v2 on v1

v2 whole, which is shorter than its diff:
```python
import functools
import math

import jax
import jax.numpy as jnp
from jax import lax
from jax.experimental import pallas as pl
from jax.experimental.pallas import tpu as pltpu
from jax.sharding import PartitionSpec as P

BLK = 128
PAIR = 2 * BLK
D = 128
HEADS = 8
WIDE = HEADS * D
COLS = 2 * HEADS * BLK
NEGATIVE = -1e30
FACTOR = 1.0 / math.sqrt(D)
TO_EXP2 = FACTOR * math.log2(math.e)
MESH = pl.DeviceIdType.MESH
F32 = jnp.float32
BF16 = jnp.bfloat16
SCORE_UNROLL = 4
GRAD_UNROLL = 4
QUERY_UNROLL = 4


def dot_last(a, b):
    return lax.dot_general(a, b, (((1,), (1,)), ((), ())), preferred_element_type=F32)


def dot_mid(a, b):
    return lax.dot_general(a, b, (((1,), (0,)), ((), ())), preferred_element_type=F32)


def rows_of(j, half):
    if j == 0 and half == 1:
        return BLK, BLK
    if j == 3 and half == 0:
        return 0, BLK
    return 0, PAIR


def position(count, inner):
    device = lax.axis_index("outer") * inner + lax.axis_index("inner")
    core = lax.rem(device, 2)
    worker = lax.div(device, 2) + core * (count - 1 - 2 * lax.div(device, 2))
    return device, core, worker


def keeps_first(order_ref, device, core, count):
    low_first = (order_ref[2 * device] < count).astype(jnp.int32)
    return jnp.full((1, 1), low_first + core) == 1


def choose(flag, first, second):
    return jnp.where(flag, first, second), jnp.where(flag, second, first)


def main_kernel(
    count,
    inner,
    order_ref,
    docs_ref,
    q_ref,
    k_ref,
    v_ref,
    do_ref,
    dq_mine,
    dq_other,
    own_grad,
    sib_grad,
    g_mine,
    g_other,
    q_in,
    do_in,
    k_in,
    v_in,
    docs_in,
    q_all,
    do_all,
    q_other,
    do_other,
    kv,
    kv_other,
    bias,
    weights,
    grad_prob,
    st_max,
    st_sum,
    st_dot,
    st_scale,
    st_row,
    probs,
    grads,
    key_t,
    g_part,
    g_send,
    g_recv,
    own_keep,
    sib_send,
    dq_send,
    in_sem,
    kv_send_sem,
    kv_recv_sem,
    sib_send_sem,
    sib_recv_sem,
    g_send_sem,
    g_recv_sem,
    out_sem,
):
    device, core, worker = position(count, inner)
    mirror = count - 1 - worker

    def place(u):
        u = lax.rem(u + count, count)
        upper = lax.div(u, count // 2)
        return 2 * u + upper * (2 * count - 1 - 4 * u)

    def coords(dev):
        return (lax.div(dev, inner), lax.rem(dev, inner))

    after = place(worker + 1)
    before = place(worker - 1)
    across = place(mirror + 1)
    sibling = place(mirror)

    first_row = jnp.maximum(2 * worker - 6, 0)
    loads = [
        pltpu.make_async_copy(k_ref, k_in, in_sem.at[0]),
        pltpu.make_async_copy(v_ref, v_in, in_sem.at[1]),
        pltpu.make_async_copy(q_ref, q_in, in_sem.at[2]),
        pltpu.make_async_copy(do_ref, do_in, in_sem.at[3]),
        pltpu.make_async_copy(docs_ref.at[pl.ds(first_row, 8)], docs_in, in_sem.at[4]),
    ]
    for load in loads:
        load.start()

    barrier = pltpu.get_barrier_semaphore()
    for dev in (after, before, sibling):
        pl.semaphore_signal(barrier, inc=1, device_id=coords(dev), device_id_type=MESH)

    @pl.when(across != device)
    def _():
        pl.semaphore_signal(barrier, inc=1, device_id=coords(across), device_id_type=MESH)

    flag = keeps_first(order_ref, device, core, count)
    loads[0].wait()
    loads[1].wait()
    for lanes, ref in ((slice(0, D), k_in), (slice(D, 2 * D), v_in)):
        mine, other = choose(flag, ref[:BLK], ref[BLK:])
        kv[3 * PAIR : 3 * PAIR + BLK, lanes] = mine
        kv_other[:, lanes] = other

    pl.semaphore_wait(barrier, 4 - (across == device).astype(jnp.int32))

    def remote(src, dst, send_sem, recv_sem, dev):
        return pltpu.make_async_remote_copy(
            src_ref=src,
            dst_ref=dst,
            send_sem=send_sem,
            recv_sem=recv_sem,
            device_id=coords(dev),
            device_id_type=MESH,
        )

    def block_rows(k, half):
        return kv.at[pl.ds((3 - k) * PAIR + half * BLK, BLK)]

    def kv_copy(k, half):
        if half and k == 1:
            src, dev = kv_other, across
        else:
            src, dev = block_rows(k - 1, half), after
        index = 2 * k + half
        return remote(src, block_rows(k, half), kv_send_sem.at[index], kv_recv_sem.at[index], dev)

    def to_sibling(src, dst, index):
        return remote(src, dst, sib_send_sem.at[index], sib_recv_sem.at[index], sibling)

    kv_copy(1, 0).start()

    @pl.when(across != device)
    def _():
        kv_copy(1, 1).start()

    @pl.when(across == device)
    def _():
        pltpu.make_async_copy(kv_other, block_rows(1, 1), kv_recv_sem.at[3]).start()

    kv_move = to_sibling(kv_other, block_rows(0, 1), 4)
    kv_move.start()

    loads[2].wait()
    loads[3].wait()
    for h in range(HEADS):
        lanes = slice(h * D, (h + 1) * D)
        rows = slice(h * BLK, (h + 1) * BLK)
        q_all[rows], q_other[rows] = choose(flag, q_in[:BLK, lanes], q_in[BLK:, lanes])
        do_all[rows], do_other[rows] = choose(flag, do_in[:BLK, lanes], do_in[BLK:, lanes])
    q_move = to_sibling(q_other, q_all.at[pl.ds(COLS // 2, COLS // 2)], 0)
    do_move = to_sibling(do_other, do_all.at[pl.ds(COLS // 2, COLS // 2)], 1)
    q_move.start()
    do_move.start()

    loads[4].wait()
    key_iota = lax.broadcasted_iota(jnp.int32, (BLK, BLK), 0)
    query_iota = lax.broadcasted_iota(jnp.int32, (BLK, BLK), 1)

    def doc_row(window_block):
        block = 2 * worker - 6 + window_block
        return docs_in[jnp.maximum(block, 0) - first_row]

    def make_masks(blocks):
        query_docs = [jnp.broadcast_to(doc_row(6 + half), (BLK, BLK)) for half in (0, 1)]
        for block in blocks:
            key_docs = jnp.broadcast_to(doc_row(block).astype(F32), (BLK, BLK)).T.astype(jnp.int32)
            key_docs = jnp.where(2 * worker - 6 + block >= 0, key_docs, -1)
            for half in (0, 1):
                if block < half or block > 6 + half:
                    continue
                allowed = key_docs == query_docs[half]
                if block == 6 + half:
                    allowed = allowed & (key_iota <= query_iota)
                if block == half:
                    allowed = allowed & (key_iota > query_iota)
                bias[half, block * BLK : (block + 1) * BLK] = jnp.where(allowed, 0.0, NEGATIVE)

    def scores(j, half):
        first, rows = rows_of(j, half)
        begin = j * PAIR + first

        def step(i, carry):
            t = half * 4 + i
            lanes = pl.ds(pl.multiple_of(t * PAIR, PAIR), PAIR)
            mask = bias[half, begin : begin + rows]
            s = dot_last(kv[begin : begin + rows, :D], q_all[lanes])
            s = s + jnp.concatenate([mask, mask], 1)
            g = dot_last(kv[begin : begin + rows, D:], do_all[lanes])
            top = jnp.max(s, axis=0, keepdims=True)
            e = jnp.exp2((s - top) * TO_EXP2)
            weights[j, t, first : first + rows] = e
            grad_prob[j, t, first : first + rows] = g
            st_max[j, t] = jnp.broadcast_to(top, (8, PAIR))
            st_sum[j, t] = jnp.sum(e.reshape(rows // 8, 8, PAIR), axis=0)
            st_dot[j, t] = jnp.sum((e * g).reshape(rows // 8, 8, PAIR), axis=0)
            return carry

        lax.fori_loop(0, 4, step, 0, unroll=SCORE_UNROLL)

    def transpose_keys(j):
        begin = j * PAIR
        key_t[:, begin : begin + PAIR] = kv[begin : begin + PAIR, :D].astype(F32).T.astype(BF16)

    def pass_on(k):
        for half in (0, 1):
            kv_copy(k, half).wait_recv()
            kv_copy(k + 1, half).start()

    make_masks((6, 7))
    scores(3, 0)
    kv_move.wait_recv()
    make_masks((4, 5))
    pass_on(1)
    transpose_keys(3)
    q_move.wait_recv()
    do_move.wait_recv()
    scores(3, 1)
    scores(2, 0)
    pass_on(2)
    make_masks((0, 1, 2, 3))
    scores(2, 1)
    transpose_keys(2)
    scores(1, 0)
    scores(1, 1)
    transpose_keys(1)
    kv_copy(3, 0).wait_recv()
    kv_copy(3, 1).wait_recv()
    scores(0, 0)
    scores(0, 1)

    def finish_stats(t, carry):
        tops = [st_max[j, t] for j in range(4)]
        top = jnp.maximum(jnp.maximum(tops[0], tops[1]), jnp.maximum(tops[2], tops[3]))
        scales = [jnp.exp2((tops[j] - top) * TO_EXP2) for j in range(4)]
        total = sum(st_sum[j, t] * scales[j] for j in range(4))
        dotted = sum(st_dot[j, t] * scales[j] for j in range(4))
        inverse = 1.0 / jnp.sum(total, axis=0, keepdims=True)
        row = jnp.sum(dotted, axis=0, keepdims=True) * inverse
        for j in range(4):
            st_scale[j, t] = scales[j] * inverse
        st_row[t] = jnp.broadcast_to(row, (8, PAIR))
        return carry

    lax.fori_loop(0, 8, finish_stats, 0, unroll=4)

    def grads_of(j):
        for half in (0, 1):
            first, rows = rows_of(j, half)

            def step(i, carry):
                t = half * 4 + i
                lanes = pl.ds(pl.multiple_of(t * PAIR, PAIR), PAIR)
                tall = (rows // 8, 8, PAIR)
                p = weights[j, t, first : first + rows].reshape(tall) * st_scale[j, t][None]
                g = grad_prob[j, t, first : first + rows].reshape(tall) - st_row[t][None]
                ds = (p * g).reshape(rows, PAIR)
                probs[first : first + rows, lanes] = p.reshape(rows, PAIR).astype(BF16)
                grads[j * PAIR + first : j * PAIR + first + rows, lanes] = ds.astype(BF16)
                return carry

            lax.fori_loop(0, 4, step, 0, unroll=GRAD_UNROLL)

    def key_value_grads(j, half):
        lane, lanes = 0, COLS
        if j == 0 and half == 0:
            lanes = COLS // 2
        if j == 3 and half == 1:
            lane, lanes = COLS // 2, COLS // 2
        first = half * BLK
        begin = j * PAIR + first
        gk = dot_mid(grads[begin : begin + BLK, lane : lane + lanes], q_all[lane : lane + lanes])
        gv = dot_mid(probs[first : first + BLK, lane : lane + lanes], do_all[lane : lane + lanes])
        return gk, gv

    def g_copy(k, half):
        if k > 1:
            dst, dev = g_recv.at[k - 2, half], before
        else:
            dst, dev = (g_other, across) if half else (g_mine, before)
        index = 2 * (k - 1) + half
        return remote(g_send.at[k - 1, half], dst, g_send_sem.at[index], g_recv_sem.at[index], dev)

    grads_of(0)
    for half in (0, 1):
        gk, gv = key_value_grads(0, half)
        g_send[2, half, :, :D] = gk.astype(BF16)
        g_send[2, half, :, D:] = gv.astype(BF16)
        g_copy(3, half).start()

    def part_of(k):
        grads_of(3 - k)
        for half in (0, 1):
            gk, gv = key_value_grads(3 - k, half)
            g_part[k - 1, half, :, :D] = gk
            g_part[k - 1, half, :, D:] = gv

    def add_and_send(k):
        for half in (0, 1):
            g_copy(k + 1, half).wait_recv()
            total = g_part[k - 1, half] + g_recv[k - 1, half].astype(F32)
            g_send[k - 1, half] = total.astype(BF16)
            if k == 1 and half == 1:

                @pl.when(across != device)
                def _():
                    g_copy(1, 1).start()

                @pl.when(across == device)
                def _():
                    pltpu.make_async_copy(g_send.at[0, 1], g_other, g_recv_sem.at[1]).start()
            else:
                g_copy(k, half).start()

    def query_grads(half, emit):
        begin = half * BLK

        def step(i, carry):
            lanes = pl.ds(pl.multiple_of((half * 4 + i) * PAIR, PAIR), PAIR)
            g = dot_mid(key_t[:, begin : begin + 7 * BLK], grads[begin : begin + 7 * BLK, lanes])
            g = g * FACTOR
            for side in (0, 1):
                head = pl.ds(pl.multiple_of((i * 2 + side) * D, D), D)
                dq_send[half, :, head] = g[:, side * BLK : (side + 1) * BLK].T.astype(BF16)
            return carry

        lax.fori_loop(0, 4, step, 0, unroll=QUERY_UNROLL)

    part_of(2)
    part_of(1)
    add_and_send(2)
    transpose_keys(0)
    grads_of(3)
    gk, gv = key_value_grads(3, 1)
    sib_send[:, :D] = gk
    sib_send[:, D:] = gv
    sib_move = to_sibling(sib_send, sib_grad, 2)
    sib_move.start()
    gk, gv = key_value_grads(3, 0)
    own_keep[:, :D] = gk
    own_keep[:, D:] = gv
    own_out = pltpu.make_async_copy(own_keep, own_grad, out_sem.at[0])
    own_out.start()
    query_grads(1, None)
    dq_move = to_sibling(dq_send.at[1], dq_other, 3)
    dq_move.start()
    add_and_send(1)
    query_grads(0, None)
    dq_out = pltpu.make_async_copy(dq_send.at[0], dq_mine, out_sem.at[1])
    dq_out.start()

    own_out.wait()
    for move in (q_move, do_move, kv_move, sib_move, dq_move):
        move.wait_send()
    for k in (1, 2, 3):
        for half in (0, 1):
            if k == 1 and half == 1:

                @pl.when(across != device)
                def _():
                    kv_copy(1, 1).wait_send()
                    g_copy(1, 1).wait_send()
            else:
                kv_copy(k, half).wait_send()
                g_copy(k, half).wait_send()
    sib_move.wait_recv()
    dq_out.wait()
    dq_move.wait_recv()
    g_copy(1, 0).wait_recv()
    g_copy(1, 1).wait_recv()


def last_kernel(
    count,
    inner,
    order_ref,
    dq_mine,
    dq_other,
    own_grad,
    sib_grad,
    g_mine,
    g_other,
    dq_ref,
    dk_ref,
    dv_ref,
):
    device, core, _ = position(count, inner)
    flag = keeps_first(order_ref, device, core, count)
    dq_ref[:BLK], dq_ref[BLK:] = choose(flag, dq_mine[...], dq_other[...])
    mine = own_grad[...] + g_mine[...].astype(F32)
    other = sib_grad[...] + g_other[...].astype(F32)
    one, two = choose(flag, mine, other)
    dk_ref[:BLK] = (one[:, :D] * FACTOR).astype(BF16)
    dk_ref[BLK:] = (two[:, :D] * FACTOR).astype(BF16)
    dv_ref[:BLK] = one[:, D:].astype(BF16)
    dv_ref[BLK:] = two[:, D:].astype(BF16)


def on_device(queries, key_states, value_states, grad_output, documents, block_order):
    inner = lax.axis_size("inner")
    count = lax.axis_size("outer") * inner
    smem = pl.BlockSpec(memory_space=pltpu.SMEM)
    vmem = pl.BlockSpec(memory_space=pltpu.VMEM)
    hbm = pl.BlockSpec(memory_space=pl.ANY)
    docs = documents.reshape(2 * count, 1, BLK)
    mid = pl.pallas_call(
        functools.partial(main_kernel, count, inner),
        out_shape=[
            jax.ShapeDtypeStruct((BLK, WIDE), BF16),
            jax.ShapeDtypeStruct((BLK, WIDE), BF16),
            jax.ShapeDtypeStruct((BLK, 2 * D), F32),
            jax.ShapeDtypeStruct((BLK, 2 * D), F32),
            jax.ShapeDtypeStruct((BLK, 2 * D), BF16),
            jax.ShapeDtypeStruct((BLK, 2 * D), BF16),
        ],
        in_specs=[smem] + [hbm] * 5,
        out_specs=[hbm] * 6,
        scratch_shapes=[
            pltpu.VMEM((PAIR, WIDE), BF16),
            pltpu.VMEM((PAIR, WIDE), BF16),
            pltpu.VMEM((PAIR, D), BF16),
            pltpu.VMEM((PAIR, D), BF16),
            pltpu.VMEM((8, 1, BLK), jnp.int32),
            pltpu.VMEM((COLS, D), BF16),
            pltpu.VMEM((COLS, D), BF16),
            pltpu.VMEM((COLS // 2, D), BF16),
            pltpu.VMEM((COLS // 2, D), BF16),
            pltpu.VMEM((4 * PAIR, 2 * D), BF16),
            pltpu.VMEM((BLK, 2 * D), BF16),
            pltpu.VMEM((2, 4 * PAIR, BLK), F32),
            pltpu.VMEM((4, 8, PAIR, PAIR), F32),
            pltpu.VMEM((4, 8, PAIR, PAIR), F32),
            pltpu.VMEM((4, 8, 8, PAIR), F32),
            pltpu.VMEM((4, 8, 8, PAIR), F32),
            pltpu.VMEM((4, 8, 8, PAIR), F32),
            pltpu.VMEM((4, 8, 8, PAIR), F32),
            pltpu.VMEM((8, 8, PAIR), F32),
            pltpu.VMEM((PAIR, COLS), BF16),
            pltpu.VMEM((4 * PAIR, COLS), BF16),
            pltpu.VMEM((D, 4 * PAIR), BF16),
            pltpu.VMEM((2, 2, BLK, 2 * D), F32),
            pltpu.VMEM((3, 2, BLK, 2 * D), BF16),
            pltpu.VMEM((2, 2, BLK, 2 * D), BF16),
            pltpu.VMEM((BLK, 2 * D), F32),
            pltpu.VMEM((BLK, 2 * D), F32),
            pltpu.VMEM((2, BLK, WIDE), BF16),
            pltpu.SemaphoreType.DMA((5,)),
            pltpu.SemaphoreType.DMA((8,)),
            pltpu.SemaphoreType.DMA((8,)),
            pltpu.SemaphoreType.DMA((5,)),
            pltpu.SemaphoreType.DMA((5,)),
            pltpu.SemaphoreType.DMA((6,)),
            pltpu.SemaphoreType.DMA((6,)),
            pltpu.SemaphoreType.DMA((2,)),
        ],
        compiler_params=pltpu.CompilerParams(
            collective_id=0, has_side_effects=True, vmem_limit_bytes=60 * 1024 * 1024
        ),
        name="attention_backward",
    )(block_order, docs, queries, key_states, value_states, grad_output)
    return pl.pallas_call(
        functools.partial(last_kernel, count, inner),
        out_shape=[
            jax.ShapeDtypeStruct((PAIR, WIDE), BF16),
            jax.ShapeDtypeStruct((PAIR, D), BF16),
            jax.ShapeDtypeStruct((PAIR, D), BF16),
        ],
        in_specs=[smem] + [vmem] * 6,
        out_specs=[vmem] * 3,
        name="stored_order",
    )(block_order, *mid)


def solution(mesh):
    rows = P(("outer", "inner"), None)
    return jax.shard_map(
        on_device,
        mesh=mesh,
        in_specs=(rows, rows, rows, rows, P(), P()),
        out_specs=(rows, rows, rows),
        check_vma=False,
    )
```

time: 49.9 us -> 39.5 us (0.79)
  the two profiles are of different devices: /device:TPU:1 before, /device:TPU:9 now
where the time goes in v2:
time: 39.5 us; the launch traced here: 39.3 us
  Pallas kernels  38.6 us (98%)
  between operations  0.64 us (2%)
    pallas_call x1, Pallas kernels, on_device(): pl.pallas_call(functools.partial(main_kernel, count, inner), out_shape=[j...  36.6 us
    pallas_call x1, Pallas kernels, on_device(): pl.pallas_call(functools.partial(last_kernel, count, inner), out_shape=[j...  2.03 us

profile of v2, /device:TPU:9, one launch (start us, length us, event | category | flops | bytes accessed | tf_op | source)
XLA Modules:
  0.0 39.3 jit_solution(4972366135692136395)
XLA Ops:
  0.6 36.6 %attention_backward.1 = (bf16[128,1024]{1,0:T(8,128)(2,1)}, bf16[128,1024]{1,0:T(8,128)(2,1)}, f32[128,256]{1,0:T(8,128)}, f32[128,256]{1,0:T(8,128)}, bf16[128,...) custom-call(s32[1536]{0:T(1024)} %order_ref.3, s32[1536,1,128]{2,1,0:T(1,128)} %bitcast.1, bf16[256,1024]{1,0:T(8,128)(2,1)} %q_ref.1, ...), custom_call_target="tpu_custom_call" | custom-call | tf_op jit(solution)/shard_map/attention_backward/pallas_call | solution.py:456
  37.3 2.0 %stored_order.1 = (bf16[256,1024]{1,0:T(8,128)(2,1)}, bf16[256,128]{1,0:T(8,128)(2,1)}, bf16[256,128]{1,0:T(8,128)(2,1)}) custom-call(s32[1536]{0:T(1024)} %order_ref.3, bf16[128,1024]{1,0:T(8,128)(2,1)} %get-tuple-element.9.dq_mine, bf16[128,1024]{1,0:T(8,128)(2,1)} %get-tuple-element.10.dq_other, f32[128,256]{1,0:T(8,128)} %get-tuple-element.11.own_grad, ...), custom_call_target="tpu_custom_call" | custom-call | tf_op jit(solution)/shard_map/stored_order/pallas_call | solution.py:511

commit v3 on v2

--- a/solution.py
+++ b/solution.py
@@ -23,6 +23,8 @@
 SCORE_UNROLL = 4
 GRAD_UNROLL = 4
 QUERY_UNROLL = 4
+PIECES = 2
+PIECE = BLK // PIECES
 
 
 def dot_last(a, b):
@@ -48,9 +50,13 @@
     return device, core, worker
 
 
-def keeps_first(order_ref, device, core, count):
-    low_first = (order_ref[2 * device] < count).astype(jnp.int32)
-    return jnp.full((1, 1), low_first + core) == 1
+def order_row(order_ref, order_in, device, sem):
+    return pltpu.make_async_copy(order_ref.at[lax.div(2 * device, BLK)], order_in, sem)
+
+
+def keeps_first(order_in, device, core, count):
+    low_first = (order_in[0, lax.rem(2 * device, BLK)] < count).astype(jnp.int32)
+    return low_first + core
 
 
 def choose(flag, first, second):
@@ -100,6 +106,7 @@
     own_keep,
     sib_send,
     dq_send,
+    order_in,
     in_sem,
     kv_send_sem,
     kv_recv_sem,
@@ -132,19 +139,21 @@
         pltpu.make_async_copy(q_ref, q_in, in_sem.at[2]),
         pltpu.make_async_copy(do_ref, do_in, in_sem.at[3]),
         pltpu.make_async_copy(docs_ref.at[pl.ds(first_row, 8)], docs_in, in_sem.at[4]),
+        order_row(order_ref, order_in, device, in_sem.at[5]),
     ]
-    for load in loads:
+    for load in (loads[0], loads[1], loads[5], loads[2], loads[3], loads[4]):
         load.start()
 
     barrier = pltpu.get_barrier_semaphore()
-    for dev in (after, before, sibling):
+    for dev in (before, sibling):
         pl.semaphore_signal(barrier, inc=1, device_id=coords(dev), device_id_type=MESH)
 
     @pl.when(across != device)
     def _():
         pl.semaphore_signal(barrier, inc=1, device_id=coords(across), device_id_type=MESH)
 
-    flag = keeps_first(order_ref, device, core, count)
+    loads[5].wait()
+    flag = jnp.full((1, 1), keeps_first(order_in, device, core, count)) == 1
     loads[0].wait()
     loads[1].wait()
     for lanes, ref in ((slice(0, D), k_in), (slice(D, 2 * D), v_in)):
@@ -152,7 +161,7 @@
         kv[3 * PAIR : 3 * PAIR + BLK, lanes] = mine
         kv_other[:, lanes] = other
 
-    pl.semaphore_wait(barrier, 4 - (across == device).astype(jnp.int32))
+    pl.semaphore_wait(barrier, 3 - (across == device).astype(jnp.int32))
 
     def remote(src, dst, send_sem, recv_sem, dev):
         return pltpu.make_async_remote_copy(
@@ -164,31 +173,38 @@
             device_id_type=MESH,
         )
 
-    def block_rows(k, half):
-        return kv.at[pl.ds((3 - k) * PAIR + half * BLK, BLK)]
-
-    def kv_copy(k, half):
+    def piece_rows(k, half, piece):
+        return kv.at[pl.ds((3 - k) * PAIR + half * BLK + piece * PIECE, PIECE)]
+
+    def kv_copy(k, half, piece):
         if half and k == 1:
-            src, dev = kv_other, across
+            src, dev = kv_other.at[pl.ds(piece * PIECE, PIECE)], across
         else:
-            src, dev = block_rows(k - 1, half), after
-        index = 2 * k + half
-        return remote(src, block_rows(k, half), kv_send_sem.at[index], kv_recv_sem.at[index], dev)
+            src, dev = piece_rows(k - 1, half, piece), after
+        sems = kv_send_sem.at[k - 1, half, piece], kv_recv_sem.at[k - 1, half, piece]
+        return remote(src, piece_rows(k, half, piece), *sems, dev)
 
     def to_sibling(src, dst, index):
         return remote(src, dst, sib_send_sem.at[index], sib_recv_sem.at[index], sibling)
 
-    kv_copy(1, 0).start()
+    for piece in range(PIECES):
+        kv_copy(1, 0, piece).start()
 
     @pl.when(across != device)
     def _():
-        kv_copy(1, 1).start()
+        for piece in range(PIECES):
+            kv_copy(1, 1, piece).start()
 
     @pl.when(across == device)
     def _():
-        pltpu.make_async_copy(kv_other, block_rows(1, 1), kv_recv_sem.at[3]).start()
-
-    kv_move = to_sibling(kv_other, block_rows(0, 1), 4)
+        for piece in range(PIECES):
+            pltpu.make_async_copy(
+                kv_other.at[pl.ds(piece * PIECE, PIECE)],
+                piece_rows(1, 1, piece),
+                kv_recv_sem.at[0, 1, piece],
+            ).start()
+
+    kv_move = to_sibling(kv_other, kv.at[pl.ds(3 * PAIR + BLK, BLK)], 4)
     kv_move.start()
 
     loads[2].wait()
@@ -254,8 +270,9 @@
 
     def pass_on(k):
         for half in (0, 1):
-            kv_copy(k, half).wait_recv()
-            kv_copy(k + 1, half).start()
+            for piece in range(PIECES):
+                kv_copy(k, half, piece).wait_recv()
+                kv_copy(k + 1, half, piece).start()
 
     make_masks((6, 7))
     scores(3, 0)
@@ -274,8 +291,9 @@
     scores(1, 0)
     scores(1, 1)
     transpose_keys(1)
-    kv_copy(3, 0).wait_recv()
-    kv_copy(3, 1).wait_recv()
+    for half in (0, 1):
+        for piece in range(PIECES):
+            kv_copy(3, half, piece).wait_recv()
     scores(0, 0)
     scores(0, 1)
 
@@ -323,20 +341,24 @@
         gv = dot_mid(probs[first : first + BLK, lane : lane + lanes], do_all[lane : lane + lanes])
         return gk, gv
 
-    def g_copy(k, half):
+    def g_copy(k, half, piece):
+        rows = pl.ds(piece * PIECE, PIECE)
         if k > 1:
-            dst, dev = g_recv.at[k - 2, half], before
+            dst, dev = g_recv.at[k - 2, half, rows], before
+        elif half:
+            dst, dev = g_other.at[rows], across
         else:
-            dst, dev = (g_other, across) if half else (g_mine, before)
-        index = 2 * (k - 1) + half
-        return remote(g_send.at[k - 1, half], dst, g_send_sem.at[index], g_recv_sem.at[index], dev)
+            dst, dev = g_mine.at[rows], before
+        sems = g_send_sem.at[k - 1, half, piece], g_recv_sem.at[k - 1, half, piece]
+        return remote(g_send.at[k - 1, half, rows], dst, *sems, dev)
 
     grads_of(0)
     for half in (0, 1):
         gk, gv = key_value_grads(0, half)
         g_send[2, half, :, :D] = gk.astype(BF16)
         g_send[2, half, :, D:] = gv.astype(BF16)
-        g_copy(3, half).start()
+        for piece in range(PIECES):
+            g_copy(3, half, piece).start()
 
     def part_of(k):
         grads_of(3 - k)
@@ -347,20 +369,24 @@
 
     def add_and_send(k):
         for half in (0, 1):
-            g_copy(k + 1, half).wait_recv()
-            total = g_part[k - 1, half] + g_recv[k - 1, half].astype(F32)
-            g_send[k - 1, half] = total.astype(BF16)
-            if k == 1 and half == 1:
-
-                @pl.when(across != device)
-                def _():
-                    g_copy(1, 1).start()
-
-                @pl.when(across == device)
-                def _():
-                    pltpu.make_async_copy(g_send.at[0, 1], g_other, g_recv_sem.at[1]).start()
-            else:
-                g_copy(k, half).start()
+            for piece in range(PIECES):
+                rows = pl.ds(piece * PIECE, PIECE)
+                g_copy(k + 1, half, piece).wait_recv()
+                total = g_part[k - 1, half, rows] + g_recv[k - 1, half, rows].astype(F32)
+                g_send[k - 1, half, rows] = total.astype(BF16)
+                if k == 1 and half == 1:
+
+                    @pl.when(across != device)
+                    def _():
+                        g_copy(1, 1, piece).start()
+
+                    @pl.when(across == device)
+                    def _():
+                        pltpu.make_async_copy(
+                            g_send.at[0, 1, rows], g_other.at[rows], g_recv_sem.at[0, 1, piece]
+                        ).start()
+                else:
+                    g_copy(k, half, piece).start()
 
     def query_grads(half, emit):
         begin = half * BLK
@@ -404,20 +430,22 @@
         move.wait_send()
     for k in (1, 2, 3):
         for half in (0, 1):
-            if k == 1 and half == 1:
-
-                @pl.when(across != device)
-                def _():
-                    kv_copy(1, 1).wait_send()
-                    g_copy(1, 1).wait_send()
-            else:
-                kv_copy(k, half).wait_send()
-                g_copy(k, half).wait_send()
+            for piece in range(PIECES):
+                if k == 1 and half == 1:
+
+                    @pl.when(across != device)
+                    def _():
+                        kv_copy(1, 1, piece).wait_send()
+                        g_copy(1, 1, piece).wait_send()
+                else:
+                    kv_copy(k, half, piece).wait_send()
+                    g_copy(k, half, piece).wait_send()
     sib_move.wait_recv()
     dq_out.wait()
     dq_move.wait_recv()
-    g_copy(1, 0).wait_recv()
-    g_copy(1, 1).wait_recv()
+    for half in (0, 1):
+        for piece in range(PIECES):
+            g_copy(1, half, piece).wait_recv()
 
 
 def last_kernel(
@@ -433,26 +461,59 @@
     dq_ref,
     dk_ref,
     dv_ref,
+    dq_in,
+    near_in,
+    far_in,
+    dk_out,
+    dv_out,
+    order_in,
+    in_sem,
+    out_sem,
 ):
     device, core, _ = position(count, inner)
-    flag = keeps_first(order_ref, device, core, count)
-    dq_ref[:BLK], dq_ref[BLK:] = choose(flag, dq_mine[...], dq_other[...])
-    mine = own_grad[...] + g_mine[...].astype(F32)
-    other = sib_grad[...] + g_other[...].astype(F32)
-    one, two = choose(flag, mine, other)
-    dk_ref[:BLK] = (one[:, :D] * FACTOR).astype(BF16)
-    dk_ref[BLK:] = (two[:, :D] * FACTOR).astype(BF16)
-    dv_ref[:BLK] = one[:, D:].astype(BF16)
-    dv_ref[BLK:] = two[:, D:].astype(BF16)
+    order = order_row(order_ref, order_in, device, in_sem.at[6])
+    loads = [
+        pltpu.make_async_copy(dq_mine, dq_in.at[0], in_sem.at[0]),
+        pltpu.make_async_copy(dq_other, dq_in.at[1], in_sem.at[1]),
+        pltpu.make_async_copy(own_grad, near_in.at[0], in_sem.at[2]),
+        pltpu.make_async_copy(g_mine, far_in.at[0], in_sem.at[3]),
+        pltpu.make_async_copy(sib_grad, near_in.at[1], in_sem.at[4]),
+        pltpu.make_async_copy(g_other, far_in.at[1], in_sem.at[5]),
+    ]
+    order.start()
+    for load in loads:
+        load.start()
+    order.wait()
+    mine_slot = jnp.where(keeps_first(order_in, device, core, count) == 1, 0, 1)
+    stores = []
+    for which in (0, 1):
+        slot = mine_slot if which == 0 else 1 - mine_slot
+        rows = pl.ds(pl.multiple_of(slot * BLK, BLK), BLK)
+        loads[which].wait()
+        stores.append(pltpu.make_async_copy(dq_in.at[which], dq_ref.at[rows], out_sem.at[3 * which]))
+        stores[-1].start()
+    for which in (0, 1):
+        slot = mine_slot if which == 0 else 1 - mine_slot
+        rows = pl.ds(pl.multiple_of(slot * BLK, BLK), BLK)
+        loads[2 + 2 * which].wait()
+        loads[3 + 2 * which].wait()
+        total = near_in[which] + far_in[which].astype(F32)
+        dk_out[which] = (total[:, :D] * FACTOR).astype(BF16)
+        dv_out[which] = total[:, D:].astype(BF16)
+        for step, (src, dst) in enumerate(((dk_out, dk_ref), (dv_out, dv_ref))):
+            sem = out_sem.at[3 * which + 1 + step]
+            stores.append(pltpu.make_async_copy(src.at[which], dst.at[rows], sem))
+            stores[-1].start()
+    for store in stores:
+        store.wait()
 
 
 def on_device(queries, key_states, value_states, grad_output, documents, block_order):
     inner = lax.axis_size("inner")
     count = lax.axis_size("outer") * inner
-    smem = pl.BlockSpec(memory_space=pltpu.SMEM)
-    vmem = pl.BlockSpec(memory_space=pltpu.VMEM)
     hbm = pl.BlockSpec(memory_space=pl.ANY)
     docs = documents.reshape(2 * count, 1, BLK)
+    order = block_order.reshape(2 * count // BLK, 1, BLK)
     mid = pl.pallas_call(
         functools.partial(main_kernel, count, inner),
         out_shape=[
@@ -463,7 +524,7 @@
             jax.ShapeDtypeStruct((BLK, 2 * D), BF16),
             jax.ShapeDtypeStruct((BLK, 2 * D), BF16),
         ],
-        in_specs=[smem] + [hbm] * 5,
+        in_specs=[hbm] * 6,
         out_specs=[hbm] * 6,
         scratch_shapes=[
             pltpu.VMEM((PAIR, WIDE), BF16),
@@ -494,20 +555,21 @@
             pltpu.VMEM((BLK, 2 * D), F32),
             pltpu.VMEM((BLK, 2 * D), F32),
             pltpu.VMEM((2, BLK, WIDE), BF16),
-            pltpu.SemaphoreType.DMA((5,)),
-            pltpu.SemaphoreType.DMA((8,)),
-            pltpu.SemaphoreType.DMA((8,)),
+            pltpu.SMEM((1, BLK), jnp.int32),
+            pltpu.SemaphoreType.DMA((6,)),
+            pltpu.SemaphoreType.DMA((3, 2, PIECES)),
+            pltpu.SemaphoreType.DMA((3, 2, PIECES)),
             pltpu.SemaphoreType.DMA((5,)),
             pltpu.SemaphoreType.DMA((5,)),
-            pltpu.SemaphoreType.DMA((6,)),
-            pltpu.SemaphoreType.DMA((6,)),
+            pltpu.SemaphoreType.DMA((3, 2, PIECES)),
+            pltpu.SemaphoreType.DMA((3, 2, PIECES)),
             pltpu.SemaphoreType.DMA((2,)),
         ],
         compiler_params=pltpu.CompilerParams(
             collective_id=0, has_side_effects=True, vmem_limit_bytes=60 * 1024 * 1024
         ),
         name="attention_backward",
-    )(block_order, docs, queries, key_states, value_states, grad_output)
+    )(order, docs, queries, key_states, value_states, grad_output)
     return pl.pallas_call(
         functools.partial(last_kernel, count, inner),
         out_shape=[
@@ -515,10 +577,20 @@
             jax.ShapeDtypeStruct((PAIR, D), BF16),
             jax.ShapeDtypeStruct((PAIR, D), BF16),
         ],
-        in_specs=[smem] + [vmem] * 6,
-        out_specs=[vmem] * 3,
+        in_specs=[hbm] * 7,
+        out_specs=[hbm] * 3,
+        scratch_shapes=[
+            pltpu.VMEM((2, BLK, WIDE), BF16),
+            pltpu.VMEM((2, BLK, 2 * D), F32),
+            pltpu.VMEM((2, BLK, 2 * D), BF16),
+            pltpu.VMEM((2, BLK, D), BF16),
+            pltpu.VMEM((2, BLK, D), BF16),
+            pltpu.SMEM((1, BLK), jnp.int32),
+            pltpu.SemaphoreType.DMA((7,)),
+            pltpu.SemaphoreType.DMA((6,)),
+        ],
         name="stored_order",
-    )(block_order, *mid)
+    )(order, *mid)
 
 
 def solution(mesh):

time: 39.5 us -> 38.2 us (0.967)
  the two profiles are of different devices: /device:TPU:9 before, /device:TPU:1 now
where the time goes in v3:
time: 38.2 us; the launch traced here: 38 us
  Pallas kernels  36.1 us (95%)
  local copies, waits for them, and re-layouts  1.3 us (3%)
  between operations  0.64 us (2%)
    pallas_call x1, Pallas kernels, on_device(): pl.pallas_call(functools.partial(main_kernel, count, inner), out_shape=[j...  34.2 us
    pallas_call x1, Pallas kernels, on_device(): pl.pallas_call(functools.partial(last_kernel, count, inner), out_shape=[j...  1.91 us
    reshape x1, local copies, waits for them, and re-layouts, on_device(): order = block_order.reshape(2 * count // BLK, 1, BLK)  1.3 us

profile of v3, /device:TPU:1, one launch (start us, length us, event | category | flops | bytes accessed | tf_op | source)
XLA Modules:
  0.0 38.0 jit_solution(5541696475203931326)
XLA Ops:
  0.6 1.3 %reshape.12.order_ref = s32[12,1,128]{2,1,0:T(1,128)} reshape(s32[1536]{0:T(1024)} %param.11) | data formatting | bytes 12288 | tf_op jit(solution)/shard_map/reshape | solution.py:516
  1.9 34.2 %attention_backward.1 = (bf16[128,1024]{1,0:T(8,128)(2,1)}, bf16[128,1024]{1,0:T(8,128)(2,1)}, f32[128,256]{1,0:T(8,128)}, f32[128,256]{1,0:T(8,128)}, bf16[128,...) custom-call(s32[12,1,128]{2,1,0:T(1,128)} %reshape.12.order_ref, s32[1536,1,128]{2,1,0:T(1,128)} %bitcast.1, ...), custom_call_target="tpu_custom_call" | custom-call | tf_op jit(solution)/shard_map/attention_backward/pallas_call | solution.py:517
  36.1 1.9 %stored_order.1 = (bf16[256,1024]{1,0:T(8,128)(2,1)}, bf16[256,128]{1,0:T(8,128)(2,1)}, bf16[256,128]{1,0:T(8,128)(2,1)}) custom-call(s32[12,1,128]{2,1,0:T(1,128)} %reshape.12.order_ref, bf16[128,1024]{1,0:T(8,128)(2,1)} %get-tuple-element.9.dq_mine, bf16[128,1024]{1,0:T(8,128)(2,1)} %get-tuple-element.10.dq_other, f32[128,256]{1,0:T(8,128)} %get-tuple-element.11.own_grad, ...), custom_call_target="tpu_custom_call" | custom-call | tf_op jit(solution)/shard_map/stored_order/pallas_call | solution.py:573

commit v4 on v3

--- a/solution.py
+++ b/solution.py
@@ -50,12 +50,8 @@
     return device, core, worker
 
 
-def order_row(order_ref, order_in, device, sem):
-    return pltpu.make_async_copy(order_ref.at[lax.div(2 * device, BLK)], order_in, sem)
-
-
 def keeps_first(order_in, device, core, count):
-    low_first = (order_in[0, lax.rem(2 * device, BLK)] < count).astype(jnp.int32)
+    low_first = (order_in[2 * device] < count).astype(jnp.int32)
     return low_first + core
 
 
@@ -107,6 +103,7 @@
     sib_send,
     dq_send,
     order_in,
+    nothing,
     in_sem,
     kv_send_sem,
     kv_recv_sem,
@@ -131,6 +128,9 @@
     before = place(worker - 1)
     across = place(mirror + 1)
     sibling = place(mirror)
+    has_after = worker < count - 1
+    reaches_across = (worker > 0) & (worker != count // 2)
+    keeps_across = worker == count // 2
 
     first_row = jnp.maximum(2 * worker - 6, 0)
     loads = [
@@ -139,16 +139,19 @@
         pltpu.make_async_copy(q_ref, q_in, in_sem.at[2]),
         pltpu.make_async_copy(do_ref, do_in, in_sem.at[3]),
         pltpu.make_async_copy(docs_ref.at[pl.ds(first_row, 8)], docs_in, in_sem.at[4]),
-        order_row(order_ref, order_in, device, in_sem.at[5]),
+        pltpu.make_async_copy(order_ref, order_in, in_sem.at[5]),
     ]
     for load in (loads[0], loads[1], loads[5], loads[2], loads[3], loads[4]):
         load.start()
 
     barrier = pltpu.get_barrier_semaphore()
-    for dev in (before, sibling):
-        pl.semaphore_signal(barrier, inc=1, device_id=coords(dev), device_id_type=MESH)
-
-    @pl.when(across != device)
+    pl.semaphore_signal(barrier, inc=1, device_id=coords(sibling), device_id_type=MESH)
+
+    @pl.when(worker > 0)
+    def _():
+        pl.semaphore_signal(barrier, inc=1, device_id=coords(before), device_id_type=MESH)
+
+    @pl.when(reaches_across)
     def _():
         pl.semaphore_signal(barrier, inc=1, device_id=coords(across), device_id_type=MESH)
 
@@ -161,7 +164,7 @@
         kv[3 * PAIR : 3 * PAIR + BLK, lanes] = mine
         kv_other[:, lanes] = other
 
-    pl.semaphore_wait(barrier, 3 - (across == device).astype(jnp.int32))
+    pl.semaphore_wait(barrier, 1 + has_after.astype(jnp.int32) + reaches_across.astype(jnp.int32))
 
     def remote(src, dst, send_sem, recv_sem, dev):
         return pltpu.make_async_remote_copy(
@@ -187,15 +190,17 @@
     def to_sibling(src, dst, index):
         return remote(src, dst, sib_send_sem.at[index], sib_recv_sem.at[index], sibling)
 
-    for piece in range(PIECES):
-        kv_copy(1, 0, piece).start()
-
-    @pl.when(across != device)
+    @pl.when(has_after)
+    def _():
+        for piece in range(PIECES):
+            kv_copy(1, 0, piece).start()
+
+    @pl.when(reaches_across)
     def _():
         for piece in range(PIECES):
             kv_copy(1, 1, piece).start()
 
-    @pl.when(across == device)
+    @pl.when(keeps_across)
     def _():
         for piece in range(PIECES):
             pltpu.make_async_copy(
@@ -203,6 +208,39 @@
                 piece_rows(1, 1, piece),
                 kv_recv_sem.at[0, 1, piece],
             ).start()
+
+    nothing[...] = jnp.zeros_like(nothing)
+    for k in (1, 2, 3):
+
+        @pl.when(worker < k)
+        def _():
+            for half in (0, 1):
+                for piece in range(PIECES):
+                    pltpu.make_async_copy(
+                        nothing, piece_rows(k, half, piece), kv_recv_sem.at[k - 1, half, piece]
+                    ).start()
+
+    pieces = [pl.ds(piece * PIECE, PIECE) for piece in range(PIECES)]
+
+    @pl.when(worker == count - 1)
+    def _():
+        for piece, rows in enumerate(pieces):
+            pltpu.make_async_copy(nothing, g_mine.at[rows], g_recv_sem.at[0, 0, piece]).start()
+
+    for k in (2, 3):
+
+        @pl.when((worker == count - 1) | (worker < k - 1))
+        def _():
+            for half in (0, 1):
+                for piece, rows in enumerate(pieces):
+                    pltpu.make_async_copy(
+                        nothing, g_recv.at[k - 2, half, rows], g_recv_sem.at[k - 1, half, piece]
+                    ).start()
+
+    @pl.when(worker == 0)
+    def _():
+        for piece, rows in enumerate(pieces):
+            pltpu.make_async_copy(nothing, g_other.at[rows], g_recv_sem.at[0, 1, piece]).start()
 
     kv_move = to_sibling(kv_other, kv.at[pl.ds(3 * PAIR + BLK, BLK)], 4)
     kv_move.start()
@@ -272,7 +310,10 @@
         for half in (0, 1):
             for piece in range(PIECES):
                 kv_copy(k, half, piece).wait_recv()
-                kv_copy(k + 1, half, piece).start()
+
+                @pl.when(has_after & (worker >= k))
+                def _():
+                    kv_copy(k + 1, half, piece).start()
 
     make_masks((6, 7))
     scores(3, 0)
@@ -357,8 +398,11 @@
         gk, gv = key_value_grads(0, half)
         g_send[2, half, :, :D] = gk.astype(BF16)
         g_send[2, half, :, D:] = gv.astype(BF16)
-        for piece in range(PIECES):
-            g_copy(3, half, piece).start()
+
+        @pl.when(worker >= 3)
+        def _():
+            for piece in range(PIECES):
+                g_copy(3, half, piece).start()
 
     def part_of(k):
         grads_of(3 - k)
@@ -376,17 +420,20 @@
                 g_send[k - 1, half, rows] = total.astype(BF16)
                 if k == 1 and half == 1:
 
-                    @pl.when(across != device)
+                    @pl.when(reaches_across)
                     def _():
                         g_copy(1, 1, piece).start()
 
-                    @pl.when(across == device)
+                    @pl.when(keeps_across)
                     def _():
                         pltpu.make_async_copy(
                             g_send.at[0, 1, rows], g_other.at[rows], g_recv_sem.at[0, 1, piece]
                         ).start()
                 else:
-                    g_copy(k, half, piece).start()
+
+                    @pl.when(worker >= k)
+                    def _():
+                        g_copy(k, half, piece).start()
 
     def query_grads(half, emit):
         begin = half * BLK
@@ -430,16 +477,20 @@
         move.wait_send()
     for k in (1, 2, 3):
         for half in (0, 1):
-            for piece in range(PIECES):
-                if k == 1 and half == 1:
-
-                    @pl.when(across != device)
-                    def _():
-                        kv_copy(1, 1, piece).wait_send()
-                        g_copy(1, 1, piece).wait_send()
-                else:
+            sends = reaches_across if k == 1 and half == 1 else worker >= k
+
+            @pl.when(sends)
+            def _():
+                for piece in range(PIECES):
+                    g_copy(k, half, piece).wait_send()
+
+            if not (k == 1 and half == 1):
+                sends = has_after & (worker >= k - 1)
+
+            @pl.when(sends)
+            def _():
+                for piece in range(PIECES):
                     kv_copy(k, half, piece).wait_send()
-                    g_copy(k, half, piece).wait_send()
     sib_move.wait_recv()
     dq_out.wait()
     dq_move.wait_recv()
@@ -471,7 +522,7 @@
     out_sem,
 ):
     device, core, _ = position(count, inner)
-    order = order_row(order_ref, order_in, device, in_sem.at[6])
+    order = pltpu.make_async_copy(order_ref, order_in, in_sem.at[6])
     loads = [
         pltpu.make_async_copy(dq_mine, dq_in.at[0], in_sem.at[0]),
         pltpu.make_async_copy(dq_other, dq_in.at[1], in_sem.at[1]),
@@ -513,7 +564,6 @@
     count = lax.axis_size("outer") * inner
     hbm = pl.BlockSpec(memory_space=pl.ANY)
     docs = documents.reshape(2 * count, 1, BLK)
-    order = block_order.reshape(2 * count // BLK, 1, BLK)
     mid = pl.pallas_call(
         functools.partial(main_kernel, count, inner),
         out_shape=[
@@ -555,7 +605,8 @@
             pltpu.VMEM((BLK, 2 * D), F32),
             pltpu.VMEM((BLK, 2 * D), F32),
             pltpu.VMEM((2, BLK, WIDE), BF16),
-            pltpu.SMEM((1, BLK), jnp.int32),
+            pltpu.SMEM((2 * count,), jnp.int32),
+            pltpu.VMEM((PIECE, 2 * D), BF16),
             pltpu.SemaphoreType.DMA((6,)),
             pltpu.SemaphoreType.DMA((3, 2, PIECES)),
             pltpu.SemaphoreType.DMA((3, 2, PIECES)),
@@ -569,7 +620,7 @@
             collective_id=0, has_side_effects=True, vmem_limit_bytes=60 * 1024 * 1024
         ),
         name="attention_backward",
-    )(order, docs, queries, key_states, value_states, grad_output)
+    )(block_order, docs, queries, key_states, value_states, grad_output)
     return pl.pallas_call(
         functools.partial(last_kernel, count, inner),
         out_shape=[
@@ -585,12 +636,12 @@
             pltpu.VMEM((2, BLK, 2 * D), BF16),
             pltpu.VMEM((2, BLK, D), BF16),
             pltpu.VMEM((2, BLK, D), BF16),
-            pltpu.SMEM((1, BLK), jnp.int32),
+            pltpu.SMEM((2 * count,), jnp.int32),
             pltpu.SemaphoreType.DMA((7,)),
             pltpu.SemaphoreType.DMA((6,)),
         ],
         name="stored_order",
-    )(order, *mid)
+    )(block_order, *mid)
 
 
 def solution(mesh):

time: 38.2 us -> 37.1 us (0.971)
  local copies, waits for them, and re-layouts: 1.3 us -> 0 us
    reshape x1 -> x0, local copies, waits for them, and re-layouts: 1.3 us -> none  [on_device(): order = block_order.reshape(2 * count // BLK, 1, BLK)]
where the time goes in v4:
time: 37.1 us; the launch traced here: 36.9 us
  Pallas kernels  36.3 us (98%)
  between operations  0.64 us (2%)
    pallas_call x1, Pallas kernels, on_device(): pl.pallas_call(functools.partial(main_kernel, count, inner), out_shape=[j...  34.4 us
    pallas_call x1, Pallas kernels, on_device(): pl.pallas_call(functools.partial(last_kernel, count, inner), out_shape=[j...  1.89 us

profile of v4, /device:TPU:1, one launch (start us, length us, event | category | flops | bytes accessed | tf_op | source)
XLA Modules:
  0.0 36.9 jit_solution(3480178108606760881)
XLA Ops:
  0.6 34.4 %attention_backward.1 = (bf16[128,1024]{1,0:T(8,128)(2,1)}, bf16[128,1024]{1,0:T(8,128)(2,1)}, f32[128,256]{1,0:T(8,128)}, f32[128,256]{1,0:T(8,128)}, bf16[128,...) custom-call(s32[1536]{0:T(1024)} %order_ref.3, s32[1536,1,128]{2,1,0:T(1,128)} %bitcast.1, bf16[256,1024]{1,0:T(8,128)(2,1)} %q_ref.1, ...), custom_call_target="tpu_custom_call" | custom-call | tf_op jit(solution)/shard_map/attention_backward/pallas_call | solution.py:567
  35.0 1.9 %stored_order.1 = (bf16[256,1024]{1,0:T(8,128)(2,1)}, bf16[256,128]{1,0:T(8,128)(2,1)}, bf16[256,128]{1,0:T(8,128)(2,1)}) custom-call(s32[1536]{0:T(1024)} %order_ref.3, bf16[128,1024]{1,0:T(8,128)(2,1)} %get-tuple-element.9.dq_mine, bf16[128,1024]{1,0:T(8,128)(2,1)} %get-tuple-element.10.dq_other, f32[128,256]{1,0:T(8,128)} %get-tuple-element.11.own_grad, ...), custom_call_target="tpu_custom_call" | custom-call | tf_op jit(solution)/shard_map/stored_order/pallas_call | solution.py:624

commit v5 on v4

--- a/solution.py
+++ b/solution.py
@@ -353,8 +353,8 @@
 
     lax.fori_loop(0, 8, finish_stats, 0, unroll=4)
 
-    def grads_of(j):
-        for half in (0, 1):
+    def grads_of(j, halves=(0, 1)):
+        for half in halves:
             first, rows = rows_of(j, half)
 
             def step(i, carry):
@@ -393,8 +393,8 @@
         sems = g_send_sem.at[k - 1, half, piece], g_recv_sem.at[k - 1, half, piece]
         return remote(g_send.at[k - 1, half, rows], dst, *sems, dev)
 
-    grads_of(0)
     for half in (0, 1):
+        grads_of(0, (half,))
         gk, gv = key_value_grads(0, half)
         g_send[2, half, :, :D] = gk.astype(BF16)
         g_send[2, half, :, D:] = gv.astype(BF16)

time: 37.1 us -> 36.8 us (level)
  no operation moved by 1% of the time
where the time goes in v5:
time: 36.8 us; the launch traced here: 36.6 us
  Pallas kernels  36 us (98%)
  between operations  0.64 us (2%)
    pallas_call x1, Pallas kernels, on_device(): pl.pallas_call(functools.partial(main_kernel, count, inner), out_shape=[j...  34.1 us
    pallas_call x1, Pallas kernels, on_device(): pl.pallas_call(functools.partial(last_kernel, count, inner), out_shape=[j...  1.89 us

profile of v5, /device:TPU:1, one launch (start us, length us, event | category | flops | bytes accessed | tf_op | source)
XLA Modules:
  0.0 36.6 jit_solution(3867005938634216310)
XLA Ops:
  0.6 34.1 %attention_backward.1 = (bf16[128,1024]{1,0:T(8,128)(2,1)}, bf16[128,1024]{1,0:T(8,128)(2,1)}, f32[128,256]{1,0:T(8,128)}, f32[128,256]{1,0:T(8,128)}, bf16[128,...) custom-call(s32[1536]{0:T(1024)} %order_ref.3, s32[1536,1,128]{2,1,0:T(1,128)} %bitcast.1, bf16[256,1024]{1,0:T(8,128)(2,1)} %q_ref.1, ...), custom_call_target="tpu_custom_call" | custom-call | tf_op jit(solution)/shard_map/attention_backward/pallas_call | solution.py:567
  34.7 1.9 %stored_order.1 = (bf16[256,1024]{1,0:T(8,128)(2,1)}, bf16[256,128]{1,0:T(8,128)(2,1)}, bf16[256,128]{1,0:T(8,128)(2,1)}) custom-call(s32[1536]{0:T(1024)} %order_ref.3, bf16[128,1024]{1,0:T(8,128)(2,1)} %get-tuple-element.9.dq_mine, bf16[128,1024]{1,0:T(8,128)(2,1)} %get-tuple-element.10.dq_other, f32[128,256]{1,0:T(8,128)} %get-tuple-element.11.own_grad, ...), custom_call_target="tpu_custom_call" | custom-call | tf_op jit(solution)/shard_map/stored_order/pallas_call | solution.py:624
